TPU v7x, 128 devices: a whole 4x4x4 slice. The times are simulated.
128 devices in a mesh: dp: 32 (over z, x, core), section: 4 (over y).
Axes of the slice: x: 4, y: 4, z: 4, core: 2. Of those that a mesh axis runs over, the one named last changes fastest.
Arguments:
- tokens: bfloat16 [128, 197, 768], P(('dp', 'section')), may hold values from -6 to 6
- masked: int32 [128, 197], P(('dp', 'section')), may hold values from 0 to 1, as said below
- live_images: int32 [32], replicated, may hold values from 2 to 4, as said below
- mask_token: bfloat16 [768], replicated, may hold values from -5 to 5
- norm_gain: float32 [4, 768], P('section'), may hold values from 0.1 to 1.9
- norm_shift: float32 [4, 768], P('section'), may hold values from -3 to 3
- w_first: bfloat16 [4, 768, 3072], P('section')
- w_second: bfloat16 [2, 3072, 768], replicated, may hold values from -0.109375 to 0.109375
- layer_scale: float32 [4, 768], P('section'), may hold values from 0.5 to 2
- rel_table: float32 [2, 732, 12], replicated, may hold values from -4 to 4
- cotangent: bfloat16 [128, 197, 768], P(('dp', 'section')), may hold values from -6 to 6
Outputs:
- block_out: bfloat16 [128, 197, 768], P(('dp', 'section'))
- tokens_grad: bfloat16 [128, 197, 768], P(('dp', 'section'))
- first_grad: float32 [4, 768, 3072], P('section')
- second_grad: float32 [2, 3072, 768], P(None, ('dp', 'section'))
- gain_grad: float32 [4, 768], P('section')
- shift_grad: float32 [4, 768], P('section')
- scale_grad: float32 [4, 768], P('section')
- table_grad: float32 [2, 732, 12], replicated
- mask_grad: float32 [768], replicated
- rms_out: float32 [4, 2], replicated
Inputs may be any that keep to these rules, and one draw needn't show every extreme that they name: The class token (position 0) of every image is never masked. `live_images`: images in use of the 4 slots of one index of dp; the unused slots are the last ones of that index; some index is full.
All inputs are finite; a program needn't handle non-finite values.
Results may differ from a plain program's by a relative error of at most 0.025.
Values may be sent and summed in bfloat16 or wider, within the bound.
A program may use at most 512 MiB of HBM per device.

v0:
```python
import math

import jax
import jax.numpy as jnp
from jax import lax
from jax.sharding import PartitionSpec as P

GRID = 14


EPSILON = 1e-06
SQRT_HALF = 0.7071067811865476
INV_ROOT_TWO_PI = 0.3989422804014327
HIGH = lax.Precision.HIGHEST


def from_behind(array, axis, by):
    count = lax.axis_size(axis)
    pairs = [(i, i + by) for i in range(count) if 0 <= i + by < count]
    return lax.ppermute(array, axis, pairs)


def normalize(residual, gain_vec, shift_vec):
    average = jnp.mean(residual, axis=-1, keepdims=True)
    centred = residual - average
    inv_std = lax.rsqrt(jnp.mean(centred * centred, axis=-1, keepdims=True) + EPSILON)
    scaled = centred * inv_std
    return (scaled * gain_vec + shift_vec, scaled, inv_std)


def norm_back(grad_normed, scaled, inv_std, gain_vec):
    grad_scaled = grad_normed * gain_vec
    first_mean = jnp.mean(grad_scaled, axis=-1, keepdims=True)
    second_mean = jnp.mean(grad_scaled * scaled, axis=-1, keepdims=True)
    grad_input = inv_std * (grad_scaled - first_mean - scaled * second_mean)
    return (grad_input, jnp.sum(grad_normed * scaled, axis=0), jnp.sum(grad_normed, axis=0))


def gelu_slope(pre_act):
    return (
        0.5 * (1.0 + lax.erf(pre_act * SQRT_HALF))
        + pre_act * jnp.exp(-0.5 * pre_act * pre_act) * INV_ROOT_TWO_PI
    )


def expand_bias(bias_table):
    head_count = bias_table.shape[1]
    span_size = 2 * GRID - 1
    core_grid = bias_table[: span_size * span_size].reshape(span_size, span_size, head_count)
    positions = jnp.arange(GRID)
    offsets = positions[:, None] - positions[None, :] + GRID - 1
    select = (offsets[None, :, :] == jnp.arange(span_size)[:, None, None]).astype(jnp.float32)
    halfway = jnp.einsum("bxj,abh->axjh", select, core_grid, precision=HIGH)
    patch_bias = jnp.einsum("ayz,axjh->hyxzj", select, halfway, precision=HIGH)
    patches = GRID * GRID
    patch_bias = patch_bias.reshape(head_count, patches, patches)
    corner = bias_table[span_size * span_size + 2][:, None, None]
    first_row = jnp.broadcast_to(
        bias_table[span_size * span_size][:, None, None], (head_count, 1, patches)
    )
    left_column = jnp.broadcast_to(
        bias_table[span_size * span_size + 1][:, None, None], (head_count, patches, 1)
    )
    top_rows = jnp.concatenate([corner, first_row], axis=2)
    other_rows = jnp.concatenate([left_column, patch_bias], axis=2)
    return jnp.concatenate([top_rows, other_rows], axis=1)


def on_device(
    tokens,
    masked,
    live_images,
    mask_token,
    norm_gain,
    norm_shift,
    w_first,
    w_second,
    layer_scale,
    rel_table,
    cotangent,
):
    sections = lax.axis_size("section")
    section_index = lax.axis_index("section")
    img_count = tokens.shape[0]
    seq_len = tokens.shape[1]
    model_width = tokens.shape[2]
    hidden_width = w_first.shape[2]
    head_count = rel_table.shape[2]
    table_rows = rel_table.shape[1]
    layers = w_second.shape[0]
    head_size = model_width // head_count
    inv_root = 1.0 / math.sqrt(head_size)
    row_count = img_count * seq_len
    steps_total = 2 * sections - 1
    lse_shape = (img_count, head_count, seq_len)
    is_masked = (masked == 1)[:, :, None]
    started = jnp.where(is_masked, mask_token[None, None, :], tokens)
    all_inputs, all_cotangents = (
        lax.all_gather(started, "section", axis=0, tiled=True),
        lax.all_gather(cotangent, "section", axis=0, tiled=True),
    )
    live_here = lax.dynamic_index_in_dim(live_images, lax.axis_index("dp"), keepdims=False)
    slot_valid = (
        (jnp.arange(sections * img_count) < live_here)
        .astype(jnp.float32)
        .reshape(sections, img_count)
    )
    parity = section_index % 2
    layer_index = section_index // 2
    weights_in = w_first[0]
    gain_vec = norm_gain[0]
    shift_vec = norm_shift[0]
    scale_vec = layer_scale[0]
    bias_table = lax.dynamic_index_in_dim(rel_table, layer_index, keepdims=False)
    down_proj = lax.dynamic_index_in_dim(w_second, layer_index, keepdims=False)
    position_bias = expand_bias(bias_table)

    def row_validity(batch_index, active):
        clipped = jnp.clip(batch_index, 0, sections - 1)
        picked = lax.dynamic_index_in_dim(slot_valid, clipped, keepdims=False)
        widened = jnp.broadcast_to(picked[:, None], (img_count, seq_len)).reshape(row_count)
        return widened * jnp.asarray(active).astype(jnp.float32)

    def split_heads(packed):
        shaped = packed.reshape(img_count, seq_len, 3, head_count, head_size)
        return (shaped[:, :, 0], shaped[:, :, 1], shaped[:, :, 2])

    def attn_scores(query_part, key_part):
        return (
            jnp.einsum("bqhd,bkhd->bhqk", query_part, key_part, preferred_element_type=jnp.float32)
            * inv_root
            + position_bias[None]
        )

    def blank_forward(resid_in):
        return (
            jnp.zeros((row_count, model_width), jnp.float32),
            jnp.zeros((row_count, model_width), jnp.float32),
            jnp.zeros((row_count, hidden_width), jnp.float32),
            jnp.zeros(lse_shape, jnp.float32),
        )

    def attend_forward(resid_in):
        residual = resid_in.astype(jnp.float32)
        normed, _, _ = normalize(residual, gain_vec, shift_vec)
        normed_low = normed.astype(jnp.bfloat16)
        packed = jnp.dot(
            normed_low, weights_in[:, : 3 * model_width], preferred_element_type=jnp.float32
        ).astype(jnp.bfloat16)
        query_part, key_part, value_part = split_heads(packed)
        scores = attn_scores(query_part, key_part)
        row_peak = jnp.max(scores, axis=-1, keepdims=True)
        exp_scores = jnp.exp(scores - row_peak)
        row_total = jnp.sum(exp_scores, axis=-1, keepdims=True)
        attn_probs = (exp_scores / row_total).astype(jnp.bfloat16)
        mixed_heads = jnp.einsum(
            "bhqk,bkhd->bqhd", attn_probs, value_part, preferred_element_type=jnp.float32
        )
        mixed_heads = mixed_heads.reshape(row_count, model_width).astype(jnp.bfloat16)
        projected = jnp.dot(
            mixed_heads, weights_in[:, 3 * model_width :], preferred_element_type=jnp.float32
        )
        result = residual + scale_vec * projected
        middle = jnp.concatenate([packed, mixed_heads], axis=1).astype(jnp.float32)
        log_total = (row_peak + jnp.log(row_total))[..., 0]
        return (result, projected, middle, log_total)

    def dense_forward(resid_in):
        residual = resid_in.astype(jnp.float32)
        normed, _, _ = normalize(residual, gain_vec, shift_vec)
        normed_low = normed.astype(jnp.bfloat16)
        pre_act = jnp.dot(normed_low, weights_in, preferred_element_type=jnp.float32)
        activated = jax.nn.gelu(pre_act, approximate=False).astype(jnp.bfloat16)
        projected = jnp.dot(activated, down_proj, preferred_element_type=jnp.float32)
        result = residual + scale_vec * projected
        return (result, projected, pre_act, jnp.zeros(lse_shape, jnp.float32))

    def blank_backward(resid_in, projected, middle, log_total, grad_out):
        return (
            jnp.zeros((row_count, model_width), jnp.float32),
            jnp.zeros((model_width, hidden_width), jnp.float32),
            jnp.zeros((hidden_width, model_width), jnp.float32),
            jnp.zeros((model_width,), jnp.float32),
            jnp.zeros((model_width,), jnp.float32),
            jnp.zeros((model_width,), jnp.float32),
            jnp.zeros((table_rows, head_count), jnp.float32),
        )

    def attend_backward(resid_in, projected, middle, log_total, grad_out):
        residual = resid_in.astype(jnp.float32)
        normed, scaled, inv_std = normalize(residual, gain_vec, shift_vec)
        normed_low = normed.astype(jnp.bfloat16)
        packed = middle[:, : 3 * model_width].astype(jnp.bfloat16)
        mixed_heads = middle[:, 3 * model_width :].astype(jnp.bfloat16)
        query_part, key_part, value_part = split_heads(packed)
        attn_probs = jnp.exp(attn_scores(query_part, key_part) - log_total[..., None])
        probs_low = attn_probs.astype(jnp.bfloat16)
        scale_grad = jnp.sum(grad_out * projected, axis=0)
        grad_proj = (scale_vec * grad_out).astype(jnp.bfloat16)
        out_weight_grad = jnp.einsum(
            "rd,re->de", mixed_heads, grad_proj, preferred_element_type=jnp.float32
        )
        grad_mixed = jnp.einsum(
            "re,de->rd",
            grad_proj,
            weights_in[:, 3 * model_width :],
            preferred_element_type=jnp.float32,
        )
        grad_mixed = grad_mixed.astype(jnp.bfloat16).reshape(
            img_count, seq_len, head_count, head_size
        )
        grad_probs = jnp.einsum(
            "bqhd,bkhd->bhqk", grad_mixed, value_part, preferred_element_type=jnp.float32
        )
        grad_value = jnp.einsum(
            "bhqk,bqhd->bkhd", probs_low, grad_mixed, preferred_element_type=jnp.float32
        )
        inner_sum = jnp.sum(grad_probs * attn_probs, axis=-1, keepdims=True)
        grad_scores = (attn_probs * (grad_probs - inner_sum)).astype(jnp.bfloat16)
        bias_grad = jnp.sum(grad_scores.astype(jnp.float32), axis=0)
        _, expand_back = jax.vjp(expand_bias, bias_table)
        table_grad = expand_back(bias_grad)[0]
        grad_query = (
            jnp.einsum("bhqk,bkhd->bqhd", grad_scores, key_part, preferred_element_type=jnp.float32)
            * inv_root
        )
        grad_key = (
            jnp.einsum(
                "bhqk,bqhd->bkhd", grad_scores, query_part, preferred_element_type=jnp.float32
            )
            * inv_root
        )
        grad_packed = (
            jnp.stack([grad_query, grad_key, grad_value], axis=2)
            .reshape(row_count, 3 * model_width)
            .astype(jnp.bfloat16)
        )
        qkv_weight_grad = jnp.einsum(
            "rd,re->de", normed_low, grad_packed, preferred_element_type=jnp.float32
        )
        grad_normed = jnp.einsum(
            "re,de->rd",
            grad_packed,
            weights_in[:, : 3 * model_width],
            preferred_element_type=jnp.float32,
        )
        grad_input, gain_grad, shift_grad = norm_back(grad_normed, scaled, inv_std, gain_vec)
        first_grad = jnp.concatenate([qkv_weight_grad, out_weight_grad], axis=1)
        return (
            grad_out + grad_input,
            first_grad,
            jnp.zeros((hidden_width, model_width), jnp.float32),
            gain_grad,
            shift_grad,
            scale_grad,
            table_grad,
        )

    def dense_backward(resid_in, projected, middle, log_total, grad_out):
        residual = resid_in.astype(jnp.float32)
        normed, scaled, inv_std = normalize(residual, gain_vec, shift_vec)
        normed_low = normed.astype(jnp.bfloat16)
        activated = jax.nn.gelu(middle, approximate=False).astype(jnp.bfloat16)
        scale_grad = jnp.sum(grad_out * projected, axis=0)
        grad_proj = (scale_vec * grad_out).astype(jnp.bfloat16)
        down_grad = jnp.einsum(
            "rf,rd->fd", activated, grad_proj, preferred_element_type=jnp.float32
        )
        grad_act = jnp.einsum("rd,fd->rf", grad_proj, down_proj, preferred_element_type=jnp.float32)
        grad_pre = (grad_act * gelu_slope(middle)).astype(jnp.bfloat16)
        up_grad = jnp.einsum("rd,rf->df", normed_low, grad_pre, preferred_element_type=jnp.float32)
        grad_normed = jnp.einsum(
            "rf,df->rd", grad_pre, weights_in, preferred_element_type=jnp.float32
        )
        grad_input, gain_grad, shift_grad = norm_back(grad_normed, scaled, inv_std, gain_vec)
        return (
            grad_out + grad_input,
            up_grad,
            down_grad,
            gain_grad,
            shift_grad,
            scale_grad,
            jnp.zeros((table_rows, head_count), jnp.float32),
        )

    forwards = [blank_forward, attend_forward, dense_forward]
    backwards = [blank_backward, attend_backward, dense_backward]
    incoming = jnp.zeros((row_count, model_width), jnp.bfloat16)
    kept_state = []
    finals = []
    branch_square = jnp.zeros((), jnp.float32)
    resid_square = jnp.zeros((), jnp.float32)
    for time_step in range(steps_total):
        batch_index = time_step - section_index
        active = (batch_index >= 0) & (batch_index < sections)
        if time_step < sections:
            fresh = all_inputs[time_step * img_count : (time_step + 1) * img_count].reshape(
                row_count, model_width
            )
            resid_in = jnp.where(section_index == 0, fresh, incoming)
        else:
            resid_in = incoming
        branch_pick = jnp.where(active, 1 + parity, 0)
        result, projected, middle, log_total = lax.switch(branch_pick, forwards, resid_in)
        row_weight = row_validity(batch_index, active)
        branch_term = scale_vec * projected
        branch_square = branch_square + jnp.sum(
            row_weight * jnp.sum(branch_term * branch_term, axis=1)
        )
        resid_square = resid_square + jnp.sum(row_weight * jnp.sum(result * result, axis=1))
        kept_state.append(resid_in)
        if time_step >= sections - 1:
            finals.append(result * row_weight[:, None])
        if time_step < steps_total - 1:
            incoming = from_behind(result.astype(jnp.bfloat16), "section", 1)
    incoming_grad = jnp.zeros((row_count, model_width), jnp.bfloat16)
    grad_sums = blank_backward(incoming_grad, None, None, None, None)[1:]
    first_outs = []
    for back_step in range(steps_total):
        time_step = steps_total - 1 - back_step
        batch_index = time_step - section_index
        active = (batch_index >= 0) & (batch_index < sections)
        branch_pick = jnp.where(active, 1 + parity, 0)
        resid_in = kept_state[time_step]
        _, projected, middle, log_total = lax.switch(branch_pick, forwards, resid_in)
        if back_step < sections:
            last_batch = sections - 1 - back_step
            fresh_grad = all_cotangents[
                last_batch * img_count : (last_batch + 1) * img_count
            ].reshape(row_count, model_width)
            fresh_grad = fresh_grad.astype(jnp.float32) * row_validity(last_batch, True)[:, None]
            grad_out = jnp.where(
                section_index == sections - 1, fresh_grad, incoming_grad.astype(jnp.float32)
            )
        else:
            grad_out = incoming_grad.astype(jnp.float32)
        pieces = lax.switch(
            branch_pick, backwards, resid_in, projected, middle, log_total, grad_out
        )
        grad_input = pieces[0]
        grad_sums = jax.tree.map(jnp.add, grad_sums, pieces[1:])
        if time_step < sections:
            first_outs.append(grad_input)
        if back_step < steps_total - 1:
            incoming_grad = from_behind(grad_input.astype(jnp.bfloat16), "section", -1)
    final_stack = jnp.stack(finals).reshape(sections * img_count, seq_len, model_width)
    grad_stack = jnp.stack(first_outs[::-1]).reshape(sections * img_count, seq_len, model_width)
    final_term = jnp.where(section_index == sections - 1, final_stack, 0.0)
    grad_term = jnp.where(section_index == 0, grad_stack, 0.0)
    own_out, own_grad = (
        lax.psum_scatter(
            final_term.astype(jnp.bfloat16), "section", scatter_dimension=0, tiled=True
        ).astype(jnp.float32),
        lax.psum_scatter(
            grad_term.astype(jnp.bfloat16), "section", scatter_dimension=0, tiled=True
        ).astype(jnp.float32),
    )
    block_out = own_out.astype(jnp.bfloat16)
    tokens_grad = jnp.where(is_masked, 0.0, own_grad).astype(jnp.bfloat16)
    mask_part = jnp.sum(jnp.where(is_masked, own_grad, 0.0), axis=(0, 1))
    up_local, down_local, gain_local, shift_local, scale_local, table_local = grad_sums
    first_total, gain_total, shift_total, scale_total = (
        lax.psum(up_local.astype(jnp.bfloat16), "dp").astype(jnp.float32),
        lax.psum(gain_local.astype(jnp.bfloat16), "dp").astype(jnp.float32),
        lax.psum(shift_local.astype(jnp.bfloat16), "dp").astype(jnp.float32),
        lax.psum(scale_local.astype(jnp.bfloat16), "dp").astype(jnp.float32),
    )
    layer_pick = (jnp.arange(layers) == layer_index).astype(jnp.float32)[:, None, None]
    placed = layer_pick * down_local[None]
    second_total = lax.psum_scatter(placed, ("dp", "section"), scatter_dimension=1, tiled=True)
    table_full = layer_pick * table_local[None]
    section_pick = (jnp.arange(sections) == section_index).astype(jnp.float32)[:, None]
    sums_full = section_pick * jnp.stack([branch_square, resid_square])[None, :]
    table_total, mask_total, sums_total = lax.psum(
        (table_full, mask_part, sums_full), ("dp", "section")
    )
    token_total = jnp.sum(live_images).astype(jnp.float32) * seq_len * model_width
    rms_out = jnp.sqrt(sums_total / token_total)
    return (
        block_out,
        tokens_grad,
        first_total[None],
        second_total,
        gain_total[None],
        shift_total[None],
        scale_total[None],
        table_total,
        mask_total,
        rms_out,
    )


def solution(mesh):
    return jax.shard_map(
        on_device,
        mesh=mesh,
        in_specs=(
            P(("dp", "section"), None, None),
            P(("dp", "section"), None),
            P(),
            P(),
            P("section", None),
            P("section", None),
            P("section", None, None),
            P(),
            P("section", None),
            P(),
            P(("dp", "section"), None, None),
        ),
        out_specs=(
            P(("dp", "section"), None, None),
            P(("dp", "section"), None, None),
            P("section", None, None),
            P(None, ("dp", "section"), None),
            P("section", None),
            P("section", None),
            P("section", None),
            P(),
            P(),
            P(),
        ),
        check_vma=False,
    )
```

profile of v0, /device:TPU:1, one launch (start us, length us, event | category | flops | bytes accessed | tf_op | source)
XLA Modules:
  0.0 1525.8 jit_solution(8034919277029269775)
XLA Ops:
  22.8 23.1 %copy.349 = f32[12,14,14,14,14]{4,3,2,1,0:T(8,128)} copy(f32[12,14,14,14,14]{3,4,1,0,2:T(8,128)} %convolution_bitcast_fusion.14) | data formatting | bytes 3687936 | tf_op jit(solution)/shard_map/ayz,axjh->hyxzj/transpose | solution.py:54
  68.9 30.8 %conditional.21 = ((f32[197,768]{1,0:T(8,128)}, f32[197,768]{1,0:T(8,128)S(1)})) conditional(s32[]{:T(128)} %clamp.17, () %tuple.266, (bf16[197,768]{1,0:T(8,128)(2,1)}, f32[1,768]{1,0:T(1,128)S(1)}, f32[1,768]{1,0:T(1,128)S(1)}, f32[1,768]{1,0:T(1,128)S(1)}, bf16[768,3072]{1,0:T(8,128)(2,1)}, ...), branch_computations={%region_0.1_spmd, %region_1.6_spmd, %region_6.9_spmd} | conditional | flops 1900731904 | bytes 34076484 | solution.py:304
  111.3 21.4 %conditional.22 = ((f32[197,768]{1,0:T(8,128)}, f32[197,768]{1,0:T(8,128)})) conditional(s32[]{:T(128)} %clamp.16, () %tuple.265, (bf16[197,768]{1,0:T(8,128)(2,1)}, f32[1,768]{1,0:T(1,128)S(1)}, f32[1,768]{1,0:T(1,128)S(1)}, f32[1,768]{1,0:T(1,128)S(1)}, bf16[768,3072]{1,0:T(8,128)(2,1)}, ...), branch_computations={%region_9.10_spmd, %region_10.15_spmd, %region_15.18_spmd} | conditional | flops 1900731904 | bytes 33985860 | solution.py:304
  142.5 22.4 %conditional.23 = ((f32[197,768]{1,0:T(8,128)}, f32[197,768]{1,0:T(8,128)S(1)})) conditional(s32[]{:T(128)} %clamp.15, () %tuple.264, (bf16[197,768]{1,0:T(8,128)(2,1)}, f32[1,768]{1,0:T(1,128)S(1)}, f32[1,768]{1,0:T(1,128)S(1)}, f32[1,768]{1,0:T(1,128)S(1)}, bf16[768,3072]{1,0:T(8,128)(2,1)}, ...), branch_computations={%region_18.19_spmd, %region_19.24_spmd, %region_24.27_spmd} | conditional | flops 1900731904 | bytes 34076484 | solution.py:304
  175.2 22.2 %conditional.24 = ((f32[197,768]{1,0:T(8,128)S(1)}, f32[197,768]{1,0:T(8,128)})) conditional(s32[]{:T(128)} %clamp.14, () %tuple.263, (bf16[197,768]{1,0:T(8,128)(2,1)}, f32[1,768]{1,0:T(1,128)S(1)}, f32[1,768]{1,0:T(1,128)S(1)}, f32[1,768]{1,0:T(1,128)S(1)}, bf16[768,3072]{1,0:T(8,128)(2,1)}, ...), branch_computations={%region_27.28_spmd, %region_28.33_spmd, %region_33.36_spmd} | conditional | flops 1900731904 | bytes 34076484 | solution.py:304
  255.9 15.5 %conditional.35 = (bf16[197,768]{1,0:T(8,128)(2,1)}, f32[768,3072]{1,0:T(8,128)}, f32[3072,768]{1,0:T(8,128)S(1)}, f32[768]{0:T(1024)}, f32[768]{0:T(1024)}, /*index=5*/f32[768]{0:T(1024)}, f32[732,12]{1,0:T(8,128)S(1)}) conditional(s32[]{:T(128)} %clamp.20, () %tuple.308, (bf16[197,768]{1,0:T(8,128)(2,1)S(1)}, ...), branch_computations={%region_127.128_spmd, %region_128.139_spmd, %region_139.147_spmd} | conditional | flops 3769386496 | bytes 115951520 | solution.py:337
  277.0 21.9 %collective-permute-done.6 = bf16[197,768]{1,0:T(8,128)(2,1)} collective-permute-done((bf16[197,768]{1,0:T(8,128)(2,1)}, bf16[197,768]{1,0:T(8,128)(2,1)}, u32[]{:S(2)}, u32[]{:S(2)}) %collective-permute-start.6) | collective-permute-done | bytes 302624 | tf_op jit(solution)/shard_map/ppermute | solution.py:20
  300.7 15.7 %conditional.36 = (bf16[197,768]{1,0:T(8,128)(2,1)}, f32[768,3072]{1,0:T(8,128)}, f32[3072,768]{1,0:T(8,128)S(1)}, f32[768]{0:T(1024)}, f32[768]{0:T(1024)}, /*index=5*/f32[768]{0:T(1024)}, f32[732,12]{1,0:T(8,128)S(1)}) conditional(s32[]{:T(128)} %clamp.19, () %tuple.304, (bf16[197,768]{1,0:T(8,128)(2,1)S(1)}, ...), branch_computations={%region_147.148_spmd, %region_148.159_spmd, %region_159.167_spmd} | conditional | flops 3769386496 | bytes 121788704 | solution.py:337
  326.5 15.4 %conditional.37 = (bf16[197,768]{1,0:T(8,128)(2,1)}, f32[768,3072]{1,0:T(8,128)}, f32[3072,768]{1,0:T(8,128)S(1)}, f32[768]{0:T(1024)}, f32[768]{0:T(1024)}, /*index=5*/f32[768]{0:T(1024)}, f32[732,12]{1,0:T(8,128)S(1)}) conditional(s32[]{:T(128)} %clamp.18, () %tuple.300, (bf16[197,768]{1,0:T(8,128)(2,1)}, ...), branch_computations={%region_167.168_spmd, %region_168.179_spmd, %region_179.187_spmd} | conditional | flops 3769386496 | bytes 121783432 | solution.py:337
  345.7 21.1 %conditional.31 = (f32[197,768]{1,0:T(8,128)S(1)}, f32[197,3072]{1,0:T(8,128)}, f32[1,12,197]{2,1,0:T(8,128)S(1)}) conditional(s32[]{:T(128)} %clamp.14, () %tuple.297, (bf16[197,768]{1,0:T(8,128)(2,1)}, f32[1,768]{1,0:T(1,128)S(1)}, f32[1,768]{1,0:T(1,128)S(1)}, bf16[768,3072]{1,0:T(8,128)(2,1)}, ...), branch_computations={%region_91.92_spmd, %region_92.97_spmd, %region_97.100_spmd} | conditional | flops 1900278016 | bytes 28154592 | solution.py:325
  366.8 106.4 %collective-permute-done.8 = bf16[197,768]{1,0:T(8,128)(2,1)} collective-permute-done((bf16[197,768]{1,0:T(8,128)(2,1)}, bf16[197,768]{1,0:T(8,128)(2,1)}, u32[]{:S(2)}, u32[]{:S(2)}) %collective-permute-start.8) | collective-permute-done | bytes 302624 | tf_op jit(solution)/shard_map/ppermute | solution.py:20
  474.9 93.7 %conditional.38 = (bf16[197,768]{1,0:T(8,128)(2,1)}, f32[768,3072]{1,0:T(8,128)}, f32[3072,768]{1,0:T(8,128)S(1)}, f32[768]{0:T(1024)}, f32[768]{0:T(1024)}, /*index=5*/f32[768]{0:T(1024)}, f32[732,12]{1,0:T(8,128)S(1)}) conditional(s32[]{:T(128)} %clamp.14, () %tuple.296, (bf16[197,768]{1,0:T(8,128)(2,1)}, ...), branch_computations={%region_187.188_spmd, %region_188.199_spmd, %region_199.207_spmd} | conditional | flops 3769386496 | bytes 121783432 | solution.py:337
  520.0 12.9 reshape.2081
  532.9 20.1 %copy.317 = bf16[12,14,14,14,14]{1,2,3,0,4:T(8,128)(2,1)} copy(bf16[12,14,14,14,14]{2,1,4,3,0:T(8,128)(2,1)} %reshape.2081) | data formatting | bytes 1843968 | tf_op jit(solution)/shard_map/cond/branch_1_fun/transpose(jvp())/reshape | solution.py:56
  572.3 21.1 %conditional.30 = (f32[197,768]{1,0:T(8,128)S(1)}, f32[197,3072]{1,0:T(8,128)}, f32[1,12,197]{2,1,0:T(8,128)S(1)}) conditional(s32[]{:T(128)} %clamp.15, () %tuple.293, (bf16[197,768]{1,0:T(8,128)(2,1)}, f32[1,768]{1,0:T(1,128)S(1)}, f32[1,768]{1,0:T(1,128)S(1)}, bf16[768,3072]{1,0:T(8,128)(2,1)}, ...), branch_computations={%region_82.83_spmd, %region_83.88_spmd, %region_88.91_spmd} | conditional | flops 1900278016 | bytes 28154592 | solution.py:325
  595.5 93.9 %conditional.39 = (bf16[197,768]{1,0:T(8,128)(2,1)}, f32[768,3072]{1,0:T(8,128)}, f32[3072,768]{1,0:T(8,128)S(1)}, f32[768]{0:T(1024)}, f32[768]{0:T(1024)}, /*index=5*/f32[768]{0:T(1024)}, f32[732,12]{1,0:T(8,128)S(1)}) conditional(s32[]{:T(128)} %clamp.15, () %tuple.292, (bf16[197,768]{1,0:T(8,128)(2,1)}, ...), branch_computations={%region_207.208_spmd, %region_208.219_spmd, %region_219.227_spmd} | conditional | flops 3769386496 | bytes 121783432 | solution.py:337
  640.5 12.9 reshape.2088
  653.4 20.5 %copy.326 = bf16[12,14,14,14,14]{1,2,3,0,4:T(8,128)(2,1)} copy(bf16[12,14,14,14,14]{2,1,4,3,0:T(8,128)(2,1)} %reshape.2088) | data formatting | bytes 1843968 | tf_op jit(solution)/shard_map/cond/branch_1_fun/transpose(jvp())/reshape | solution.py:56
  693.1 21.1 %conditional.29 = (f32[197,768]{1,0:T(8,128)S(1)}, f32[197,3072]{1,0:T(8,128)}, f32[1,12,197]{2,1,0:T(8,128)S(1)}) conditional(s32[]{:T(128)} %clamp.16, () %tuple.289, (bf16[197,768]{1,0:T(8,128)(2,1)}, f32[1,768]{1,0:T(1,128)S(1)}, f32[1,768]{1,0:T(1,128)S(1)}, bf16[768,3072]{1,0:T(8,128)(2,1)}, ...), branch_computations={%region_73.74_spmd, %region_74.79_spmd, %region_79.82_spmd} | conditional | flops 1900278016 | bytes 28154592 | solution.py:325
  716.0 93.9 %conditional.40 = (bf16[197,768]{1,0:T(8,128)(2,1)}, f32[768,3072]{1,0:T(8,128)}, f32[3072,768]{1,0:T(8,128)S(1)}, f32[768]{0:T(1024)}, f32[768]{0:T(1024)}, /*index=5*/f32[768]{0:T(1024)}, f32[732,12]{1,0:T(8,128)S(1)}) conditional(s32[]{:T(128)} %clamp.16, () %tuple.288, (bf16[197,768]{1,0:T(8,128)(2,1)}, ...), branch_computations={%region_227.228_spmd, %region_228.239_spmd, %region_239.247_spmd} | conditional | flops 3769386496 | bytes 121783432 | solution.py:337
  774.1 20.4 %copy.335 = bf16[12,14,14,14,14]{1,2,3,0,4:T(8,128)(2,1)} copy(bf16[12,14,14,14,14]{2,1,4,3,0:T(8,128)(2,1)} %reshape.2095) | data formatting | bytes 1843968 | tf_op jit(solution)/shard_map/cond/branch_1_fun/transpose(jvp())/reshape | solution.py:56
  813.7 21.1 %conditional.28 = (f32[197,768]{1,0:T(8,128)S(1)}, f32[197,3072]{1,0:T(8,128)}, f32[1,12,197]{2,1,0:T(8,128)S(1)}) conditional(s32[]{:T(128)} %clamp.17, () %tuple.285, (bf16[197,768]{1,0:T(8,128)(2,1)}, f32[1,768]{1,0:T(1,128)S(1)}, f32[1,768]{1,0:T(1,128)S(1)}, bf16[768,3072]{1,0:T(8,128)(2,1)}, ...), branch_computations={%region_64.65_spmd, %region_65.70_spmd, %region_70.73_spmd} | conditional | flops 1900278016 | bytes 28154592 | solution.py:325
  836.7 96.8 %conditional.41 = (f32[768,3072]{1,0:T(8,128)}, f32[3072,768]{1,0:T(8,128)}, f32[768]{0:T(1024)}, f32[768]{0:T(1024)}, f32[768]{0:T(1024)}, /*index=5*/f32[732,12]{1,0:T(8,128)}, bf16[1,197,768]{2,1,0:T(8,128)(2,1)S(1)}) conditional(s32[]{:T(128)} %clamp.17, () %tuple.284, (bf16[197,768]{1,0:T(8,128)(2,1)}, ...), branch_computations={%region_247.248_spmd, %region_248.259_spmd, %region_259.267_spmd} | conditional | flops 3769386496 | bytes 121784096 | solution.py:337
  883.0 12.9 reshape.2102
  895.9 20.0 %copy.344 = bf16[12,14,14,14,14]{1,2,3,0,4:T(8,128)(2,1)} copy(bf16[12,14,14,14,14]{2,1,4,3,0:T(8,128)(2,1)} %reshape.2102) | data formatting | bytes 1843968 | tf_op jit(solution)/shard_map/cond/branch_1_fun/transpose(jvp())/reshape | solution.py:56
  933.5 24.3 %fusion.2004 = bf16[1,768,3072]{2,1,0:T(8,128)(2,1)} fusion(f32[768,3072]{1,0:T(8,128)} %get-tuple-element.997, f32[768,3072]{1,0:T(8,128)} %get-tuple-element.996, f32[768,3072]{1,0:T(8,128)} %get-tuple-element.995, f32[768,3072]{1,0:T(8,128)} %get-tuple-element.994, f32[768,3072]{1,0:T(8,128)} %get-tuple-element.993, f32[768,3072]{1,0:T(8,128)} %get-tuple-element.991, ...), kind=kLoop, calls=%fused_computation.2582 | loop fusion | flops 16515072 | bytes 70778880 | tf_op jit(solution)/shard_map/broadcast_in_dim | solution.py:382
  977.0 26.5 %add_add_fusion = f32[3072,768]{1,0:T(8,128)} fusion(f32[3072,768]{1,0:T(8,128)} %get-tuple-element.1004, f32[3072,768]{1,0:T(8,128)} %copy-done.7, f32[3072,768]{1,0:T(8,128)} %copy-done.6, f32[3072,768]{1,0:T(8,128)} %copy-done.5, f32[3072,768]{1,0:T(8,128)} %copy-done.4, f32[3072,768]{1,0:T(8,128)} %copy-done.2, f32[3072,768]{1,0:T(8,128)} %copy-done.3), kind=kLoop, calls=%fused_computation.2579 | loop fusion | flops 14155776 | bytes 75497472 | tf_op jit(solution)/shard_map/add | solution.py:341
  1037.2 77.4 %all-reduce.29 = (bf16[1,768]{1,0:T(2,128)(2,1)S(1)}, bf16[1,768]{1,0:T(2,128)(2,1)S(1)}, bf16[1,768]{1,0:T(2,128)(2,1)S(1)}) all-reduce(bf16[1,768]{1,0:T(2,128)(2,1)S(1)} %broadcast_in_dim.226, bf16[1,768]{1,0:T(2,128)(2,1)S(1)} %broadcast_in_dim.228, ...), channel_id=1, replica_groups=mesh['dp'=32,'section'=4] {'dp'}, use_global_device_ids=true, to_apply=%region_270.271 | all-reduce | flops 2304 | bytes 9216 | tf_op jit(solution)/shard_map/psum | solution.py:364
  1125.6 61.8 %all-reduce.28 = (f32[768]{0:T(1024)}, f32[4,2]{0,1:T(2,128)S(1)}) all-reduce(f32[768]{0:T(1024)S(1)} %get-tuple-element.1612, f32[4,2]{0,1:T(2,128)S(1)} %broadcast_multiply_fusion.72), channel_id=1, replica_groups=mesh['dp'=32,'section'=4] {'dp','section'}, use_global_device_ids=true, to_apply=%region_275.276 | all-reduce | flops 776 | bytes 6208 | tf_op jit(solution)/shard_map/psum | solution.py:374
  1188.0 63.7 %all-reduce.35.cloned.1.call-done = f32[2,732,12]{1,0,2:T(2,128)} async-done(((f32[2,732,12]{1,0,2:T(2,128)}), f32[2,732,12]{1,0,2:T(2,128)}) %all-reduce.35.cloned.1.call-update) | async-done | bytes 70288 | tf_op jit(solution)/shard_map/psum | solution.py:374
  1251.7 23.2 %reduce-scatter.4.cloned.1.call-done = bf16[1,197,768]{2,1,0:T(8,128)(2,1)} async-done(((bf16[4,197,768]{2,1,0:T(8,128)(2,1)}), bf16[1,197,768]{2,1,0:T(8,128)(2,1)}) %reduce-scatter.4.cloned.1.call-update) | async-done | bytes 302608 | tf_op jit(solution)/shard_map/reduce_scatter | solution.py:351
  1274.9 242.0 %reduce-scatter.8.cloned.1.call-done = f32[2,24,768]{2,1,0:T(8,128)} async-done(((f32[2,3072,768]{2,1,0:T(8,128)}), f32[2,24,768]{2,1,0:T(8,128)}) %reduce-scatter.8.cloned.1.call-update) | async-done | bytes 147472 | tf_op jit(solution)/shard_map/reduce_scatter | solution.py:370
  (656 shorter events, 652.4 us)
Async XLA Ops:
  7.2 60.0 %all-gather.3.cloned.1.call-start = ((), (), s32[]{:S(2)}) async-start(), calls=%async_computation.3 | async-start | bytes 1536000 | tf_op jit(solution)/shard_map/all_gather | solution.py:99
  9.7 231.0 %all-gather.5.cloned.1.call-start = ((), (), s32[]{:S(2)}) async-start(), calls=%async_computation.5 | async-start | bytes 1536000 | tf_op jit(solution)/shard_map/all_gather | solution.py:100
  102.6 7.0 collective-permute-start
  134.7 6.1 collective-permute-start.1
  167.8 5.7 collective-permute-start.2
  169.1 947.2 %all-reduce.33.cloned.1.call-start = ((), (), s32[]{:S(2)}) async-start(), calls=%async_computation.7 | async-start | bytes 9437184 | tf_op jit(solution)/shard_map/psum | solution.py:363
  198.2 5.1 collective-permute-start.3
  203.3 20.7 %copy-start.150 = (s32[32]{0:T(128)S(1)}, s32[32]{0:T(128)}, u32[]{:S(2)}) copy-start(s32[32]{0:T(128)} %param.76) | copy-start | bytes 388
  215.7 12.0 collective-permute-start.4
  230.1 13.9 collective-permute-start.5
  271.5 27.5 %collective-permute-start.6 = (bf16[197,768]{1,0:T(8,128)(2,1)}, bf16[197,768]{1,0:T(8,128)(2,1)}, u32[]{:S(2)}, u32[]{:S(2)}) collective-permute-start(bf16[197,768]{1,0:T(8,128)(2,1)} %get-tuple-element.978), channel_id=1, source_target_pairs={{1,0},{2,1},{3,2},{5,4},{6,5},{7,6},{9,8},{10,9},{11,10},{13,12},{... | collective-permute-start | bytes 907784 | tf_op jit(solution)/shard_map/ppermute | solution.py:20
  277.0 21.9 %copy-start.36 = (f32[197,768]{1,0:T(8,128)}, f32[197,768]{1,0:T(8,128)S(1)}, u32[]{:S(2)}) copy-start(f32[197,768]{1,0:T(8,128)S(1)} %get-tuple-element.979) | copy-start | bytes 1815556
  316.4 8.3 collective-permute-start.7
  342.0 131.3 %collective-permute-start.8 = (bf16[197,768]{1,0:T(8,128)(2,1)}, bf16[197,768]{1,0:T(8,128)(2,1)}, u32[]{:S(2)}, u32[]{:S(2)}) collective-permute-start(bf16[197,768]{1,0:T(8,128)(2,1)} %get-tuple-element.982), channel_id=1, source_target_pairs={{1,0},{2,1},{3,2},{5,4},{6,5},{7,6},{9,8},{10,9},{11,10},{13,12},{... | collective-permute-start | bytes 907784 | tf_op jit(solution)/shard_map/ppermute | solution.py:20
  366.8 106.4 %copy-start.40 = (f32[197,768]{1,0:T(8,128)}, f32[197,768]{1,0:T(8,128)S(1)}, u32[]{:S(2)}) copy-start(f32[197,768]{1,0:T(8,128)S(1)} %get-tuple-element.983) | copy-start | bytes 1815556
  477.3 27.5 %copy-start.110 = (f32[197]{0:T(256)}, f32[197]{0:T(256)S(1)}, u32[]{:S(2)}) copy-start(f32[197]{0:T(256)S(1)} %broadcast_multiply_fusion.48) | copy-start | bytes 2368 | tf_op jit(solution)/shard_map/cond
  478.5 26.3 %copy-start.116 = (f32[197]{0:T(256)}, f32[197]{0:T(256)S(1)}, u32[]{:S(2)}) copy-start(f32[197]{0:T(256)S(1)} %add_rsqrt_fusion.34) | copy-start | bytes 2368 | tf_op jit(solution)/shard_map/cond
  568.7 25.8 %collective-permute-start.9 = (bf16[197,768]{1,0:T(8,128)(2,1)}, bf16[197,768]{1,0:T(8,128)(2,1)}, u32[]{:S(2)}, u32[]{:S(2)}) collective-permute-start(bf16[197,768]{1,0:T(8,128)(2,1)} %get-tuple-element.984), channel_id=1, source_target_pairs={{1,0},{2,1},{3,2},{5,4},{6,5},{7,6},{9,8},{10,9},{11,10},{13,12},{... | collective-permute-start | bytes 907784 | tf_op jit(solution)/shard_map/ppermute | solution.py:20
  597.8 27.5 %copy-start.111 = (f32[197]{0:T(256)}, f32[197]{0:T(256)S(1)}, u32[]{:S(2)}) copy-start(f32[197]{0:T(256)S(1)} %broadcast_multiply_fusion.54) | copy-start | bytes 2368 | tf_op jit(solution)/shard_map/cond
  599.0 26.3 %copy-start.117 = (f32[197]{0:T(256)}, f32[197]{0:T(256)S(1)}, u32[]{:S(2)}) copy-start(f32[197]{0:T(256)S(1)} %add_rsqrt_fusion.36) | copy-start | bytes 2368 | tf_op jit(solution)/shard_map/cond
  653.4 20.5 %copy-start.105 = (pred[27,14,14,1,1]{0,2,1,4,3:T(8,128)(4,1)S(1)}, pred[27,14,14,1,1]{0,2,1,4,3:T(8,128)(4,1)}, u32[]{:S(2)}) copy-start(pred[27,14,14,1,1]{0,2,1,4,3:T(8,128)(4,1)} %get-tuple-element.1580) | copy-start | bytes 15880 | tf_op jit(solution)/shard_map/cond
  689.4 25.6 %collective-permute-start.10 = (bf16[197,768]{1,0:T(8,128)(2,1)}, bf16[197,768]{1,0:T(8,128)(2,1)}, u32[]{:S(2)}, u32[]{:S(2)}) collective-permute-start(bf16[197,768]{1,0:T(8,128)(2,1)} %get-tuple-element.986), channel_id=1, source_target_pairs={{1,0},{2,1},{3,2},{5,4},{6,5},{7,6},{9,8},{10,9},{11,10},{13,12},{... | collective-permute-start | bytes 907784 | tf_op jit(solution)/shard_map/ppermute | solution.py:20
  718.3 27.5 %copy-start.112 = (f32[197]{0:T(256)}, f32[197]{0:T(256)S(1)}, u32[]{:S(2)}) copy-start(f32[197]{0:T(256)S(1)} %broadcast_multiply_fusion.60) | copy-start | bytes 2368 | tf_op jit(solution)/shard_map/cond
  719.5 26.3 %copy-start.118 = (f32[197]{0:T(256)}, f32[197]{0:T(256)S(1)}, u32[]{:S(2)}) copy-start(f32[197]{0:T(256)S(1)} %add_rsqrt_fusion.38) | copy-start | bytes 2368 | tf_op jit(solution)/shard_map/cond
  774.1 20.4 %copy-start.106 = (pred[27,14,14,1,1]{0,2,1,4,3:T(8,128)(4,1)S(1)}, pred[27,14,14,1,1]{0,2,1,4,3:T(8,128)(4,1)}, u32[]{:S(2)}) copy-start(pred[27,14,14,1,1]{0,2,1,4,3:T(8,128)(4,1)} %get-tuple-element.1587) | copy-start | bytes 15880 | tf_op jit(solution)/shard_map/cond
  810.0 25.7 %collective-permute-start.11 = (bf16[197,768]{1,0:T(8,128)(2,1)}, bf16[197,768]{1,0:T(8,128)(2,1)}, u32[]{:S(2)}, u32[]{:S(2)}) collective-permute-start(bf16[197,768]{1,0:T(8,128)(2,1)} %get-tuple-element.988), channel_id=1, source_target_pairs={{1,0},{2,1},{3,2},{5,4},{6,5},{7,6},{9,8},{10,9},{11,10},{13,12},{... | collective-permute-start | bytes 907784 | tf_op jit(solution)/shard_map/ppermute | solution.py:20
  839.1 29.2 %copy-start.113 = (f32[197]{0:T(256)}, f32[197]{0:T(256)S(1)}, u32[]{:S(2)}) copy-start(f32[197]{0:T(256)S(1)} %broadcast_multiply_fusion.66) | copy-start | bytes 2368 | tf_op jit(solution)/shard_map/cond
  840.3 28.0 %copy-start.119 = (f32[197]{0:T(256)}, f32[197]{0:T(256)S(1)}, u32[]{:S(2)}) copy-start(f32[197]{0:T(256)S(1)} %add_rsqrt_fusion.40) | copy-start | bytes 2368 | tf_op jit(solution)/shard_map/cond
  957.9 165.9 %reduce-scatter.6.cloned.1.call-start = ((), (), s32[]{:S(2)}) async-start(), calls=%async_computation.6 | async-start | bytes 1536000 | tf_op jit(solution)/shard_map/reduce_scatter | solution.py:354
  960.4 291.3 %all-reduce.35.cloned.1.call-start = ((), (), s32[]{:S(2)}) async-start(), calls=%async_computation.9 | async-start | bytes 147456 | tf_op jit(solution)/shard_map/psum | solution.py:374
  975.6 299.3 %reduce-scatter.4.cloned.1.call-start = ((), (), s32[]{:S(2)}) async-start(), calls=%async_computation.4 | async-start | bytes 1536000 | tf_op jit(solution)/shard_map/reduce_scatter | solution.py:351
  977.0 539.9 %reduce-scatter.8.cloned.1.call-start = ((), (), s32[]{:S(2)}) async-start(), calls=%async_computation.8 | async-start | bytes 19021824 | tf_op jit(solution)/shard_map/reduce_scatter | solution.py:370
  (99 other events, 576.8 us)
Sparse Core Ops, SparseCore 0:
  10.2 26.7 all-gather.2
  169.2 26.9 all-gather.4
  958.0 124.4 all-reduce.32
  1084.9 22.4 reduce-scatter.5
  1112.5 139.1 all-reduce.34
  1254.7 20.1 reduce-scatter.3
  1280.8 236.0 reduce-scatter.7
where the time goes:
time: 1540 us; the launch traced here: 1530 us
  waiting for transfers between devices  482 us (31%)
  local copies, waits for them, and re-layouts  327 us (21%)
  other arithmetic  227 us (15%)
  matrix products  203 us (13%)
  blocking collectives  139 us (9%)
  loops' own time  85.3 us (6%)
  starting transfers between devices  32 us (2%)
  between operations  30 us (2%)
    reduce_scatter x1, waiting for transfers between devices, on_device(): lax.psum_scatter(placed, ('dp', 'section'), scatter_dimension=1, tiled=True)  242 us
    ppermute x12, waiting for transfers between devices, from_behind(): return lax.ppermute(array, axis, pairs)  152 us
    reshape x9, local copies, waits for them, and re-layouts, expand_bias(): patch_bias = patch_bias.reshape(head_count, patches, patches)  145 us
    psum x1, blocking collectives, on_device(): lax.psum(gain_local.astype(jnp.bfloat16), 'dp').astype(jnp.float32)  77.4 us
    another operation x57, local copies, waits for them, and re-layouts  76.8 us
    psum x1, waiting for transfers between devices, on_device(): lax.psum((table_full, mask_part, sums_full), ('dp', 'section'))  63.7 us
    psum x1, blocking collectives, on_device(): lax.psum((table_full, mask_part, sums_full), ('dp', 'section'))  61.8 us
    another operation x7, loops' own time, on_device(): lax.switch(branch_pick, backwards, resid_in, projected, middle, log_total...  52.7 us
  transfers between devices with their start and end apart: 19, of which 13 were waited for; matrix products, arithmetic and copies ran while one was open for 16% of the time, Pallas kernels for 0%

commit v1 on v0

v1 whole, which is shorter than its diff:
```python
import functools
import math

import jax
import jax.numpy as jnp
import numpy as np
from jax import lax
from jax.experimental import pallas as pl
from jax.experimental.pallas import tpu as pltpu
from jax.sharding import PartitionSpec as P

SEQ, ROWS, KEYS = 197, 208, 256
D, FF, HEADS, GRID = 768, 3072, 12, 14
SPAN = 2 * GRID - 1
EPSILON = 1e-06
INV_ROOT = 0.125
INV_ROOT_TWO_PI = 0.3989422804014327
F32, BF16 = jnp.float32, jnp.bfloat16
PIECES = (3, 2, 4, 4, 4, 16, 384)


def mm(a, b):
    return lax.dot_general(a, b, (((1,), (0,)), ((), ())), preferred_element_type=F32)


def mm_nt(a, b):
    return lax.dot_general(a, b, (((1,), (1,)), ((), ())), preferred_element_type=F32)


def mm_tn(a, b):
    return lax.dot_general(a, b, (((0,), (0,)), ((), ())), preferred_element_type=F32)


def lanes(start, size):
    return pl.ds(pl.multiple_of(start, 128), size)


def token_offsets():
    patch = np.arange(SEQ - 1)
    return (patch // GRID) * SPAN + patch % GRID


def selectors():
    forward = np.zeros((384, KEYS), np.float32)
    backward = np.zeros((KEYS, 384), np.float32)
    offsets = token_offsets()
    forward[offsets, np.arange(1, SEQ)] = 1.0
    backward[np.arange(1, SEQ), offsets[-1] - offsets] = 1.0
    return jnp.asarray(forward, BF16), jnp.asarray(backward, BF16)


def centre(h):
    average = jnp.mean(h, axis=-1, keepdims=True)
    centred = h - average
    inv_std = lax.rsqrt(jnp.mean(centred * centred, axis=-1, keepdims=True) + EPSILON)
    return centred * inv_std, inv_std


def gelu_pair(u):
    size = jnp.abs(u)
    t = 1.0 / (1.0 + 0.23164189 * size)
    bell = jnp.exp(-0.5 * u * u)
    poly = t * (
        0.127414796
        + t * (-0.142248368 + t * (0.7107068705 + t * (-0.7265760135 + t * 0.5307027145)))
    )
    tail = poly * bell
    phi = jnp.where(u >= 0.0, 1.0 - tail, tail)
    return u * phi, phi + u * bell * INV_ROOT_TWO_PI


def half_mask(rows, parity):
    lane = lax.broadcasted_iota(jnp.int32, (rows, 128), 1)
    return (lane < 64) if parity == 0 else (lane >= 64)


def keep_half(block, parity):
    return jnp.where(half_mask(block.shape[0], parity), block, jnp.zeros_like(block))


class Body:
    def __init__(self, **refs):
        self.__dict__.update(refs)

    def expand_bias(self, layer):
        def head(index, _):
            base = jnp.broadcast_to(self.table[pl.ds(layer * HEADS + index, 1), :], (16, 768))
            base = pltpu.roll(base, 404, 1, stride=1, stride_axis=0)
            for yi in range(GRID):
                turned = pltpu.roll(base, SPAN * yi, 1) if yi else base
                self.unfold[1 + GRID * yi : 1 + GRID * (yi + 1), :] = turned[:GRID, :384]
            spread = self.unfold[...]
            high = spread.astype(BF16)
            low = (spread - high.astype(F32)).astype(BF16)
            select = self.select_forward[...]
            grid = mm(high, select) + mm(low, select)
            row = lax.broadcasted_iota(jnp.int32, (ROWS, KEYS), 0)
            column = lax.broadcasted_iota(jnp.int32, (ROWS, KEYS), 1)
            corner = self.corner[pl.ds(layer * HEADS + index, 1), :]
            grid = jnp.where(row == 0, corner[:, 0:1], grid)
            grid = jnp.where(column == 0, corner[:, 1:2], grid)
            grid = jnp.where((row == 0) & (column == 0), corner[:, 2:3], grid)
            self.bias[index] = jnp.where(column >= SEQ, -1e30, grid)
            return 0

        lax.fori_loop(0, HEADS, head, 0)

    def normed(self, s):
        scaled, _ = centre(self.h[s].astype(F32))
        gain = self.gain[s : s + 1, :]
        shift = self.shift[s : s + 1, :]
        self.n[...] = (scaled * gain + shift).astype(BF16)

    def finish(self, s, left, right_of):
        real = (lax.broadcasted_iota(jnp.int32, (ROWS, 1), 0) < SEQ).astype(F32) * self.valid[0:1, 0:1]

        def block(j, _):
            columns = lanes(j * 256, 256)
            projected = mm(left[...], right_of(columns))
            branch = self.scale[s : s + 1, columns] * projected
            result = self.h[s, :, columns].astype(F32) + branch
            self.p[s, :, columns] = projected.astype(BF16)
            self.small[2 * s : 2 * s + 1, columns] = jnp.sum(branch * branch * real, axis=0, keepdims=True)
            self.small[2 * s + 1 : 2 * s + 2, columns] = jnp.sum(result * result * real, axis=0, keepdims=True)
            if s < 3:
                self.h[s + 1, :, columns] = result.astype(BF16)
            else:
                self.block_out[:, columns] = (result * self.valid[0:1, 0:1]).astype(BF16)
            return 0

        lax.fori_loop(0, 3, block, 0)

    def attend_forward(self, s):
        layer = s // 2
        self.normed(s)

        def project(j, _):
            columns = lanes(j * 256, 256)
            self.qkv[layer, :ROWS, columns] = mm(self.n[...], self.w[s, :, columns]).astype(BF16)
            return 0

        lax.fori_loop(0, 9, project, 0)
        self.qkv[layer, ROWS:, :] = jnp.zeros((KEYS - ROWS, 2304), BF16)

        def pair(j, _):
            q = self.qkv[layer, :ROWS, lanes(j * 128, 128)]
            k = self.qkv[layer, :, lanes(768 + j * 128, 128)]
            v = self.qkv[layer, :, lanes(1536 + j * 128, 128)]
            mixed = jnp.zeros((ROWS, 128), F32)
            for parity in range(2):
                scores = mm_nt(keep_half(q, parity), k) * INV_ROOT + self.bias[2 * j + parity]
                peak = jnp.max(scores, axis=-1, keepdims=True)
                exps = jnp.exp(scores - peak)
                total = jnp.sum(exps, axis=-1, keepdims=True)
                probs = (exps * (1.0 / total)).astype(BF16)
                self.probs[layer, 2 * j + parity] = probs
                mixed = mixed + mm(probs, keep_half(v, parity))
            self.o[layer, :, lanes(j * 128, 128)] = mixed.astype(BF16)
            return 0

        lax.fori_loop(0, HEADS // 2, pair, 0)
        self.finish(s, self.o.at[layer], lambda c: self.w[s, :, pl.ds(pl.multiple_of(2304 + c.start, 128), 256)])

    def dense_forward(self, s):
        layer = s // 2
        self.normed(s)

        def up(j, _):
            columns = lanes(j * 256, 256)
            u = mm(self.n[...], self.w[s, :, columns])
            act, slope = gelu_pair(u)
            self.a[layer, :, columns] = act.astype(BF16)
            self.slope[layer, :, columns] = slope.astype(BF16)
            return 0

        lax.fori_loop(0, 12, up, 0)
        self.finish(s, self.a.at[layer], lambda c: self.w2[layer, :, c])

    def enter(self, s):
        g = self.g[...].astype(F32)
        row = 8 + 3 * s
        self.small[row : row + 1, :] = jnp.sum(g * self.p[s].astype(F32), axis=0, keepdims=True)
        self.dp[...] = (g * self.scale[s : s + 1, :]).astype(BF16)
        self.normed(s)

    def leave(self, s, grad, width):
        def block(j, _):
            rows = pl.ds(pl.multiple_of(j * 256, 256), 256)
            self.dn[:, lanes(j * 256, 256)] = mm_nt(grad[:, :width], self.w[s, rows, :width])
            return 0

        lax.fori_loop(0, 3, block, 0)
        scaled, inv_std = centre(self.h[s].astype(F32))
        dn = self.dn[...]
        row = 8 + 3 * s
        self.small[row + 1 : row + 2, :] = jnp.sum(dn * scaled, axis=0, keepdims=True)
        self.small[row + 2 : row + 3, :] = jnp.sum(dn, axis=0, keepdims=True)
        e = dn * self.gain[s : s + 1, :]
        mean_e = jnp.mean(e, axis=-1, keepdims=True)
        mean_ex = jnp.mean(e * scaled, axis=-1, keepdims=True)
        g = self.g[...].astype(F32) + inv_std * (e - mean_e - scaled * mean_ex)
        self.g[...] = g.astype(BF16)

    def store_first(self, stage, block, grad):
        c, a3 = block // 4, block % 4
        low = grad.astype(BF16)
        for rb in range(16):
            for route in range(3):
                first = rb * 48 + route * 16
                stage[route, c, rb // 4, rb % 4, a3] = low[first : first + 16, :]

    def first_grads(self, stage, left, right, lo, hi, shift):
        def block(j, _):
            self.store_first(stage, j, mm_tn(left[...], right[:, lanes((j - shift) * 384, 384)]))
            return 0

        lax.fori_loop(lo, hi, block, 0)

    def second_grads(self, stage, layer):
        def block(q, _):
            z, x_high = q // 2, q % 2
            grad = mm_tn(self.a[layer, :, lanes(q * 384, 384)], self.dp[...])
            for x_low in range(2):
                x = 2 * x_high + x_low
                for c in range(2):
                    for y in range(4):
                        top = ((x_low * 2 + c) * 4 + y) * 24
                        part = jnp.concatenate(
                            [grad[top : top + 24, :384], grad[top : top + 24, 384:]], axis=0
                        ).astype(BF16)
                        stage[0, c, x, y, z] = part[0:16]
                        stage[1, c, y, z, x] = part[16:32]
                        stage[2, c, z, x, y] = part[32:48]
            return 0

        lax.fori_loop(0, 8, block, 0)

    def dense_backward(self, s, stage_first, stage_second):
        layer = s // 2
        self.enter(s)
        self.second_grads(stage_second, layer)

        def down(j, _):
            columns = lanes(j * 256, 256)
            rows = pl.ds(pl.multiple_of(j * 256, 256), 256)
            da = mm_nt(self.dp[...], self.w2[layer, rows, :])
            self.du[:, columns] = (da * self.slope[layer, :, columns].astype(F32)).astype(BF16)
            return 0

        lax.fori_loop(0, 12, down, 0)
        self.first_grads(stage_first, self.n, self.du, 0, 8, 0)
        self.leave(s, self.du, FF)

    def attend_backward(self, s, stage):
        layer = s // 2
        self.enter(s)
        self.first_grads(stage, self.o.at[layer], self.dp, 6, 8, 6)

        def back(j, _):
            rows = pl.ds(pl.multiple_of(j * 256, 256), 256)
            self.do[:, lanes(j * 256, 256)] = mm_nt(self.dp[...], self.w[s, rows, 2304:]).astype(BF16)
            return 0

        lax.fori_loop(0, 3, back, 0)

        def pair(j, _):
            q = self.qkv[layer, :ROWS, lanes(j * 128, 128)]
            k = self.qkv[layer, :, lanes(768 + j * 128, 128)]
            v = self.qkv[layer, :, lanes(1536 + j * 128, 128)]
            do = self.do[:, lanes(j * 128, 128)]
            dq = jnp.zeros((ROWS, 128), F32)
            dk = jnp.zeros((KEYS, 128), F32)
            dv = jnp.zeros((KEYS, 128), F32)
            for parity in range(2):
                do_half = keep_half(do, parity)
                probs = self.probs[layer, 2 * j + parity]
                wide = probs.astype(F32)
                d_probs = mm_nt(do_half, v)
                inner = jnp.sum(d_probs * wide, axis=-1, keepdims=True)
                d_scores = (wide * (d_probs - inner)).astype(BF16)
                dv = dv + mm_tn(probs, do_half)
                dq = dq + mm(d_scores, keep_half(k, parity))
                dk = dk + mm_tn(d_scores, keep_half(q, parity))
                self.fold_bias(layer, 2 * j + parity, d_scores)
            self.du[:, lanes(j * 128, 128)] = (dq * INV_ROOT).astype(BF16)
            self.du[:, lanes(768 + j * 128, 128)] = (dk[:ROWS] * INV_ROOT).astype(BF16)
            self.du[:, lanes(1536 + j * 128, 128)] = dv[:ROWS].astype(BF16)
            return 0

        lax.fori_loop(0, HEADS // 2, pair, 0)
        self.first_grads(stage, self.n, self.du, 0, 6, 0)
        self.leave(s, self.du, 2304)

    def fold_bias(self, layer, head, d_scores):
        self.fold[:, :384] = mm(d_scores, self.select_backward[...])
        total = self.fold[1:17, :]
        for yi in range(1, GRID):
            total = total + pltpu.roll(self.fold[1 + GRID * yi : 17 + GRID * yi, :], SPAN * yi, 1)
        row = lax.broadcasted_iota(jnp.int32, (16, 768), 0)
        total = jnp.where(row < GRID, total, 0.0)
        total = pltpu.roll(total, 0, 1, stride=1, stride_axis=0)
        total = jnp.sum(total, axis=0, keepdims=True)
        wide = d_scores.astype(F32)
        corner = wide[0:1, 0:1]
        top = jnp.sum(wide[0:1, :], axis=1, keepdims=True) - corner
        side = jnp.sum(wide[:, 0:1], axis=0, keepdims=True) - corner
        lane = lax.broadcasted_iota(jnp.int32, (1, 768), 1)
        total = jnp.where(lane == 729, top, total)
        total = jnp.where(lane == 730, side, total)
        total = jnp.where(lane == 731, corner, total)
        self.small[pl.ds(24 + layer * HEADS + head, 1), :] = total


def layers_kernel(
    h0, cotangent, masked, valid, w_hbm, w2_hbm, gain, shift, scale, table, corner, select_f, select_b,
    block_out, tokens_grad, grads_hbm, small,
    w, w2, h, qkv, probs, o, a, slope, p, n, bias, unfold, fold, du, dn, dp, do, g, stage,
    load_sems, store_sems,
):
    body = Body(
        valid=valid, gain=gain, shift=shift, scale=scale, table=table, corner=corner,
        select_forward=select_f, select_backward=select_b, block_out=block_out, small=small,
        w=w, w2=w2, h=h, qkv=qkv, probs=probs, o=o, a=a, slope=slope, p=p, n=n, bias=bias,
        unfold=unfold, fold=fold, du=du, dn=dn, dp=dp, do=do, g=g,
    )
    loads = []
    for s in range(4):
        loads.append(pltpu.make_async_copy(w_hbm.at[s], w.at[s], load_sems.at[s]))
    for layer in range(2):
        loads.append(pltpu.make_async_copy(w2_hbm.at[layer], w2.at[layer], load_sems.at[4 + layer]))
    for load in loads:
        load.start()
    unfold[...] = jnp.zeros_like(unfold)
    fold[...] = jnp.zeros_like(fold)
    h[0] = h0[...]
    for s in range(4):
        if s % 2 == 0:
            body.expand_bias(s // 2)
            loads[s].wait()
            body.attend_forward(s)
        else:
            loads[s].wait()
            loads[4 + s // 2].wait()
            body.dense_forward(s)
    g[...] = (cotangent[...].astype(F32) * valid[0:1, 0:1]).astype(BF16)
    stores = {}

    def store(order, tensor):
        stores[order] = pltpu.make_async_copy(stage.at[order % 2], grads_hbm.at[tensor], store_sems.at[order % 2])
        stores[order].start()

    def free(order):
        if order - 2 in stores:
            stores.pop(order - 2).wait()

    order = 0
    for s in (3, 2, 1, 0):
        if s % 2 == 1:
            free(order), free(order + 1)
            body.dense_backward(s, stage.at[(order + 1) % 2], stage.at[order % 2])
            store(order, 4 + s // 2)
            store(order + 1, s)
            order += 2
        else:
            free(order)
            body.attend_backward(s, stage.at[order % 2])
            store(order, s)
            order += 1
    grad = g[...].astype(F32)
    here = masked[:, 0:1]
    tokens_grad[...] = (grad * (1.0 - here)).astype(BF16)
    small[20:21, :] = jnp.sum(grad * here, axis=0, keepdims=True)
    small[21:24, :] = jnp.zeros((3, 768), F32)
    for left in list(stores.values()):
        left.wait()


def layers(h0, cotangent, masked, valid, w_all, w2, gain, shift, scale, table, corner):
    select_f, select_b = selectors()
    vm = pl.BlockSpec(memory_space=pltpu.VMEM)
    hbm = pl.BlockSpec(memory_space=pl.ANY)
    V = pltpu.VMEM
    return pl.pallas_call(
        layers_kernel,
        out_shape=(
            jax.ShapeDtypeStruct((ROWS, D), BF16),
            jax.ShapeDtypeStruct((ROWS, D), BF16),
            jax.ShapeDtypeStruct((6,) + PIECES, BF16),
            jax.ShapeDtypeStruct((48, D), F32),
        ),
        in_specs=[vm, vm, vm, vm, hbm, hbm] + [vm] * 7,
        out_specs=(vm, vm, hbm, vm),
        scratch_shapes=[
            V((4, D, FF), BF16), V((2, FF, D), BF16), V((4, ROWS, D), BF16), V((2, KEYS, 2304), BF16),
            V((2, HEADS, ROWS, KEYS), BF16), V((2, ROWS, D), BF16), V((2, ROWS, FF), BF16), V((2, ROWS, FF), BF16),
            V((4, ROWS, D), BF16), V((ROWS, D), BF16), V((HEADS, ROWS, KEYS), F32), V((ROWS, 384), F32),
            V((ROWS, D), F32), V((ROWS, FF), BF16), V((ROWS, D), F32), V((ROWS, D), BF16), V((ROWS, D), BF16),
            V((ROWS, D), BF16), V((2,) + PIECES, BF16),
            pltpu.SemaphoreType.DMA((6,)), pltpu.SemaphoreType.DMA((2,)),
        ],
        compiler_params=pltpu.CompilerParams(vmem_limit_bytes=64 * 2**20),
    )(h0, cotangent, masked, valid, w_all, w2, gain, shift, scale, table, corner, select_f, select_b)


MESH = pl.DeviceIdType.MESH
AXES = ("x", "y", "z")
ROUTES = (("x", "y", "z"), ("y", "z", "x"), ("z", "x", "y"))
ORDER = (5, 3, 2, 4, 1, 0)


class Place:
    def __init__(self):
        dp = lax.axis_index("dp")
        self.at = {"z": dp // 8, "x": (dp // 2) % 4, "c": dp % 2, "y": lax.axis_index("section")}

    def go(self, axis, step):
        at = dict(self.at)
        at[axis] = (at[axis] + step) % (2 if axis == "c" else 4)
        return ((at["z"] * 4 + at["x"]) * 2 + at["c"], at["y"])

    def index(self, axis, step=0):
        return (self.at[axis] + step) % 4


def meet(place):
    barrier = pltpu.get_barrier_semaphore()
    count = 0
    for axis in AXES:
        for step in (1, 2, 3):
            pl.semaphore_signal(barrier, inc=1, device_id=place.go(axis, step), device_id_type=MESH)
            count += 1
    pl.semaphore_signal(barrier, inc=1, device_id=place.go("c", 1), device_id_type=MESH)
    pl.semaphore_wait(barrier, count + 1)


class Reduce:
    def __init__(self, place, own, pair, far, line, line_in, spot, spot_in, first_out, second_out, sems):
        self.place, self.own, self.pair, self.far, self.line, self.line_in = place, own, pair, far, line, line_in
        self.spot, self.spot_in, self.first_out, self.second_out, self.sems = spot, spot_in, first_out, second_out, sems
        self.flying = {}

    def send(self, key, src, dst, number, k, device):
        copy = pltpu.make_async_remote_copy(
            src_ref=src, dst_ref=dst, send_sem=self.sems.at[0, k, number], recv_sem=self.sems.at[1, k, number],
            device_id=device, device_id_type=MESH,
        )
        copy.start()
        self.flying[key] = copy

    def swap(self, k, theirs):
        for r in range(3):
            self.send(("c", k, r), theirs(r), self.pair.at[k, r], r, k, self.place.go("c", 1))

    def first(self, k):
        place = self.place
        for r, (axis, _, _) in enumerate(ROUTES):
            self.flying[("c", k, r)].wait_recv()

            def add(a1, _):
                self.own[k, r, a1] = (self.own[k, r, a1].astype(F32) + self.pair[k, r, a1].astype(F32)).astype(BF16)
                return 0

            lax.fori_loop(0, 4, add, 0)
            own, far = self.own.at[k, r], self.far.at[k, r]
            across, ahead, behind = place.index(axis, 2), place.index(axis, 1), place.index(axis, 3)
            up, down = place.go(axis, 1), place.go(axis, 3)
            base = 3 + 6 * r
            self.send(("fa", k, r), own.at[across, 0:2], far.at[0], base, k, up)
            self.send(("fb", k, r), own.at[across, 2:4], far.at[1], base + 1, k, down)
            self.send(("db", k, r), own.at[ahead, 2:4], far.at[2], base + 2, k, up)
            self.send(("da", k, r), own.at[behind, 0:2], far.at[3], base + 3, k, down)

    def merge(self, k):
        place = self.place
        for r, (axis, _, _) in enumerate(ROUTES):
            own, far = self.own.at[k, r], self.far.at[k, r]
            ahead, behind = place.index(axis, 1), place.index(axis, 3)
            base = 3 + 6 * r
            self.flying[("fa", k, r)].wait_recv()
            far[0] = (far[0].astype(F32) + own[ahead, 0:2].astype(F32)).astype(BF16)
            self.send(("ma", k, r), far.at[0], far.at[4], base + 4, k, place.go(axis, 1))
            self.flying[("fb", k, r)].wait_recv()
            far[1] = (far[1].astype(F32) + own[behind, 2:4].astype(F32)).astype(BF16)
            self.send(("mb", k, r), far.at[1], far.at[5], base + 5, k, place.go(axis, 3))

    def second(self, k):
        place = self.place
        for r, (axis, nxt, _) in enumerate(ROUTES):
            for name in ("db", "da", "ma", "mb"):
                self.flying[(name, k, r)].wait_recv()
            own, far = self.own.at[k, r], self.far.at[k, r]
            me = place.index(axis)
            low = own[me, 0:2].astype(F32) + far[4].astype(F32) + far[3].astype(F32)
            high = own[me, 2:4].astype(F32) + far[2].astype(F32) + far[5].astype(F32)
            line, line_in = self.line.at[k, r], self.line_in.at[k, r]
            line[0:2] = low.astype(BF16)
            line[2:4] = high.astype(BF16)
            for step in (1, 2, 3):
                self.send(("s", k, r, step), line.at[place.index(nxt, step)], line_in.at[step - 1], 21 + 3 * r + step - 1, k, place.go(nxt, step))

    def third(self, k):
        place = self.place
        for r, (_, axis, nxt) in enumerate(ROUTES):
            line, line_in, spot, spot_in = self.line.at[k, r], self.line_in.at[k, r], self.spot.at[k, r], self.spot_in.at[k, r]
            total = line[place.index(axis)].astype(F32)
            for step in (1, 2, 3):
                self.flying[("s", k, r, step)].wait_recv()
                total = total + line_in[step - 1].astype(F32)
            spot[...] = total.astype(BF16)
            for step in (1, 2, 3):
                self.send(("t", k, r, step), spot.at[place.index(nxt, step)], spot_in.at[step - 1], 30 + 3 * r + step - 1, k, place.go(nxt, step))

    def close(self, k, tensor):
        place = self.place
        for r, (_, _, axis) in enumerate(ROUTES):
            spot, spot_in = self.spot.at[k, r], self.spot_in.at[k, r]
            total = spot[place.index(axis)].astype(F32)
            for step in (1, 2, 3):
                self.flying[("t", k, r, step)].wait_recv()
                total = total + spot_in[step - 1].astype(F32)
            if tensor < 4:
                self.first_out[tensor, r] = total.astype(BF16)
            elif r == 0:
                self.second_out[tensor - 4, 0:16, :384] = total
            elif r == 1:
                self.second_out[tensor - 4, 16:24, :384] = total[0:8]
                self.second_out[tensor - 4, 0:8, 384:] = total[8:16]
            else:
                self.second_out[tensor - 4, 8:24, 384:] = total

    def drain(self):
        for copy in self.flying.values():
            copy.wait_send()


class Totals:
    def __init__(self, place, part, bufs, sems):
        self.place, self.part, self.bufs, self.sems = place, part, bufs, sems
        self.copies = []

    def send(self, src, dst, number, device):
        copy = pltpu.make_async_remote_copy(
            src_ref=src, dst_ref=dst, send_sem=self.sems.at[0, number], recv_sem=self.sems.at[1, number],
            device_id=device, device_id_type=MESH,
        )
        copy.start()
        self.copies.append(copy)
        return copy

    def start(self, small):
        me = self.place.at["c"]
        self.small = small
        self.now = [self.send(small.at[1 - me], self.bufs.at[0, 0], 0, self.place.go("c", 1))]

    def step(self, number):
        place, me = self.place, self.place.at["c"]
        for copy in self.now:
            copy.wait_recv()
        if number == 0:
            self.part[...] = self.small[me] + self.bufs[0, 0]
        else:
            axis = AXES[number - 1]
            self.bufs[number, place.at[axis]] = self.part[...]
            self.part[...] = (self.bufs[number, 0] + self.bufs[number, 1]) + (self.bufs[number, 2] + self.bufs[number, 3])
        if number < 3:
            axis = AXES[number]
            self.now = [
                self.send(self.part, self.bufs.at[number + 1, place.at[axis]], 1 + 3 * number + step - 1, place.go(axis, step))
                for step in (1, 2, 3)
            ]
            for copy in self.now:
                copy.wait_send()
        else:
            self.now = [self.send(self.part, self.bufs.at[0, 1], 10, place.go("c", 1))]

    def close(self, out):
        me = self.place.at["c"]
        for copy in self.now:
            copy.wait_recv()
        out[me] = self.part[...]
        out[1 - me] = self.bufs[0, 1]
        self.copies[0].wait_send()
        self.copies[-1].wait_send()


def reduce_kernel(
    grads, small, first_out, second_out, totals, own, pair, far, line, line_in, spot, spot_in, part, bufs,
    load_sems, sems, small_sems,
):
    place = Place()
    meet(place)
    me = place.at["c"]
    reduce = Reduce(place, own, pair, far, line, line_in, spot, spot_in, first_out, second_out, sems)
    sums = Totals(place, part, bufs, small_sems)
    sums.start(small)
    loads = []
    for k, t in enumerate(ORDER):
        loads.append([pltpu.make_async_copy(grads.at[t, r, me], own.at[k, r], load_sems.at[k, r]) for r in range(3)])
        for load in loads[-1]:
            load.start()
    stages = 5
    reduce.swap(0, lambda r: grads.at[ORDER[0], r, 1 - me])
    for time in range(6 + stages - 1):
        if time + 1 < 6:
            reduce.swap(time + 1, lambda r: grads.at[ORDER[time + 1], r, 1 - me])
        for stage in reversed(range(stages)):
            k = time - stage
            if not 0 <= k < 6:
                continue
            if stage == 0:
                for load in loads[k]:
                    load.wait()
                reduce.first(k)
            elif stage == 1:
                reduce.merge(k)
            elif stage == 2:
                reduce.second(k)
            elif stage == 3:
                reduce.third(k)
            else:
                reduce.close(k, ORDER[k])
        if time < 4:
            sums.step(time)
        elif time == 4:
            sums.close(totals)
    reduce.drain()


def reduce_all(grads, small):
    vm = pl.BlockSpec(memory_space=pltpu.VMEM)
    hbm = pl.BlockSpec(memory_space=pl.ANY)
    V = pltpu.VMEM
    return pl.pallas_call(
        reduce_kernel,
        out_shape=(
            jax.ShapeDtypeStruct((4, 3, 16, 384), BF16),
            jax.ShapeDtypeStruct((2, 24, D), F32),
            jax.ShapeDtypeStruct((2, 24, D), F32),
        ),
        in_specs=[hbm, vm],
        out_specs=(vm, vm, vm),
        scratch_shapes=[
            V((6, 3, 4, 4, 4, 16, 384), BF16), V((6, 3, 4, 4, 4, 16, 384), BF16), V((6, 3, 6, 2, 4, 16, 384), BF16),
            V((6, 3, 4, 4, 16, 384), BF16), V((6, 3, 3, 4, 16, 384), BF16),
            V((6, 3, 4, 16, 384), BF16), V((6, 3, 3, 16, 384), BF16),
            V((24, D), F32), V((4, 4, 24, D), F32),
            pltpu.SemaphoreType.DMA((6, 3)), pltpu.SemaphoreType.DMA((2, 6, 39)), pltpu.SemaphoreType.DMA((2, 11)),
        ],
        compiler_params=pltpu.CompilerParams(collective_id=1, has_side_effects=True, vmem_limit_bytes=64 * 2**20),
    )(grads, small)


class Spread:
    def __init__(self, place, sems):
        self.place, self.sems = place, sems
        self.sent = []

    def send(self, number, src, dst, device):
        copy = pltpu.make_async_remote_copy(
            src_ref=src, dst_ref=dst, send_sem=self.sems.at[0, number], recv_sem=self.sems.at[1, number],
            device_id=device, device_id_type=MESH,
        )
        copy.start()
        self.sent.append(copy)

    def wait(self, number, ref):
        pltpu.make_async_remote_copy(
            src_ref=ref, dst_ref=ref, send_sem=self.sems.at[0, number], recv_sem=self.sems.at[1, number],
            device_id=self.place.go("c", 1), device_id_type=MESH,
        ).wait_recv()

    def drain(self):
        for copy in self.sent:
            copy.wait_send()


GATHER_MESSAGES = 63


class Gather(Spread):
    def __init__(self, place, source, full, sems):
        super().__init__(place, sems)
        self.source, self.full = source, full

    def rows(self, route, step, sub=None):
        top = (0 if route == "x" else 384) + self.place.index(route, step) * 96 + self.place.at["c"] * 48
        if sub is None:
            return pl.ds(pl.multiple_of(top, 16), 48)
        return pl.ds(pl.multiple_of(top + 16 * sub, 16), 16)

    def ref(self, rel, route, step, sub=None):
        return self.full.at[self.place.index("y", rel), self.rows(route, step, sub)]

    @staticmethod
    def along_y(rel, route):
        return 2 * (rel - 1) + (route == "z")

    @staticmethod
    def in_plane(rel, route, kind):
        return 6 + 5 * (2 * (rel - 1) + (route == "z")) + kind

    @staticmethod
    def across(rel, route, step):
        return 36 + 4 * (2 * (rel - 1) + (route == "z")) + step

    def begin(self):
        for route in ("x", "z"):
            mine = self.source.at[self.rows(route, 0)]
            for step in (1, 3):
                self.send(self.along_y(4 - step, route), mine, self.ref(0, route, 0), self.place.go("y", step))

    def arrive(self, rel):
        for route in ("x", "z"):
            piece = self.ref(rel, route, 0)
            self.wait(self.along_y(rel, route), piece)
            if (rel, route) == (3, "x"):
                self.send(self.along_y(2, route), piece, piece, self.place.go("y", 1))
            if (rel, route) == (1, "z"):
                self.send(self.along_y(2, route), piece, piece, self.place.go("y", 3))
            for kind, step in ((0, 1), (1, 3)):
                self.send(self.in_plane(rel, route, kind), piece, piece, self.place.go(route, step))
            self.send(self.across(rel, route, 0), piece, piece, self.place.go("c", 1))

    def turn(self, rel):
        place = self.place
        for route in ("x", "z"):
            for kind, step in ((0, 3), (1, 1)):
                piece = self.ref(rel, route, step)
                self.wait(self.in_plane(rel, route, kind), piece)
                self.send(self.across(rel, route, step), piece, piece, place.go("c", 1))
            clockwise = 1 - 2 * place.at["c"]
            for sub, way in ((0, 1), (1, clockwise), (2, -1)):
                piece = self.ref(rel, route, 4 - way, sub)
                self.send(self.in_plane(rel, route, 2 + sub), piece, piece, place.go(route, 4 + way))

    def end(self, rel):
        for route in ("x", "z"):
            for sub in range(3):
                self.wait(self.in_plane(rel, route, 2 + sub), self.ref(rel, route, 2, sub))
            piece = self.ref(rel, route, 2)
            self.send(self.across(rel, route, 2), piece, piece, self.place.go("c", 1))

    def settle(self, rel):
        other = 1 - self.place.at["c"]
        for route in ("x", "z"):
            for step in range(4):
                top = (0 if route == "x" else 384) + self.place.index(route, step) * 96 + other * 48
                self.wait(self.across(rel, route, step), self.full.at[self.place.index("y", rel), pl.ds(pl.multiple_of(top, 16), 48)])


def gather_kernel(source, vec, full, vecs, own_sem, sems):
    place = Place()
    meet(place)
    gather = Gather(place, source, full, sems)
    mine = place.at["y"]
    vecs[mine] = vec[...]
    for step in (1, 2, 3):
        gather.send(59 + step, vec, vecs.at[mine], place.go("y", step))
    own = pltpu.make_async_copy(source, full.at[place.at["y"]], own_sem)
    own.start()
    gather.begin()
    gather.arrive(3)
    gather.arrive(1)
    gather.turn(3)
    gather.turn(1)
    gather.arrive(2)
    gather.end(3)
    gather.end(1)
    gather.turn(2)
    gather.end(2)
    for rel in (3, 1, 2):
        gather.settle(rel)
    for step in (1, 2, 3):
        gather.wait(59 + step, vecs.at[place.index("y", 4 - step)])
    own.wait()
    gather.drain()


def gather_all(source, vec):
    hbm = pl.BlockSpec(memory_space=pl.ANY)
    vm = pl.BlockSpec(memory_space=pltpu.VMEM)
    return pl.pallas_call(
        gather_kernel,
        out_shape=(jax.ShapeDtypeStruct((4, D, FF), BF16), jax.ShapeDtypeStruct((4, 8, D), F32)),
        in_specs=[hbm, vm],
        out_specs=(hbm, vm),
        scratch_shapes=[pltpu.SemaphoreType.DMA, pltpu.SemaphoreType.DMA((2, GATHER_MESSAGES))],
        compiler_params=pltpu.CompilerParams(collective_id=2, has_side_effects=True),
    )(source, vec)


class Share(Spread):
    def __init__(self, place, blocks, pieces, sems):
        super().__init__(place, sems)
        self.blocks, self.pieces = blocks, pieces

    def run(self, own_sem, out, out_sem):
        place, pieces = self.place, self.pieces
        at = place.at
        c, x, y, z = at["c"], at["x"], at["y"], at["z"]
        own = pltpu.make_async_copy(self.blocks.at[y], pieces.at[c, z, x, y], own_sem)
        own.start()
        for step in (1, 2, 3):
            self.send(step - 1, self.blocks.at[place.index("y", step)], pieces.at[c, z, x, y], place.go("y", step))
        own.wait()
        for step in (1, 2, 3):
            self.wait(step - 1, pieces.at[c, z, x, place.index("y", 4 - step)])
        low, high = pl.ds(0, 2), pl.ds(2, 2)
        for step in (1, 2, 3):
            self.send(2 + step, pieces.at[c, z, x, low], pieces.at[c, z, x, low], place.go("x", step))
            self.send(5 + step, pieces.at[c, z, x, high], pieces.at[c, z, x, high], place.go("z", step))
        for step in (1, 2, 3):
            self.wait(2 + step, pieces.at[c, z, place.index("x", 4 - step), low])
            self.wait(5 + step, pieces.at[c, place.index("z", 4 - step), x, high])
        row, column = pieces.at[c, z, :, low], pieces.at[c, :, x, high]
        for step in (1, 3, 2):
            self.send(8 + step, row, row, place.go("z", step))
            self.send(11 + step, column, column, place.go("x", step))
        self.send(15, row, row, place.go("c", 1))
        self.send(16, column, column, place.go("c", 1))
        for step in (1, 3, 2):
            row = pieces.at[c, place.index("z", 4 - step), :, low]
            self.wait(8 + step, row)
            self.send(16 + step, row, row, place.go("c", 1))
            column = pieces.at[c, :, place.index("x", 4 - step), high]
            self.wait(11 + step, column)
            self.send(19 + step, column, column, place.go("c", 1))
        first = pltpu.make_async_copy(pieces.at[c], out.at[c], out_sem)
        first.start()
        self.wait(15, pieces.at[1 - c, z, :, low])
        self.wait(16, pieces.at[1 - c, :, x, high])
        for step in (1, 3, 2):
            self.wait(16 + step, pieces.at[1 - c, place.index("z", 4 - step), :, low])
            self.wait(19 + step, pieces.at[1 - c, :, place.index("x", 4 - step), high])
        first.wait()
        rest = pltpu.make_async_copy(pieces.at[1 - c], out.at[1 - c], out_sem)
        rest.start()
        rest.wait()
        self.drain()


def share_kernel(blocks, out, pieces, own_sem, out_sem, sems):
    place = Place()
    meet(place)
    Share(place, blocks, pieces, sems).run(own_sem, out, out_sem)


def assemble_kernel(first, second, third, out):
    for route, ref in enumerate((first, second, third)):
        for c in range(2):
            for a3 in range(4):
                if route == 0:
                    piece = ref[c, a3, 0, 0, 0]
                elif route == 1:
                    piece = ref[c, 0, a3, 0, 0]
                else:
                    piece = ref[c, 0, 0, a3, 0]
                left = (c * 4 + a3) * 384
                out[16 * route : 16 * route + 16, left : left + 384] = piece.astype(F32)


def share_all(blocks):
    hbm = pl.BlockSpec(memory_space=pl.ANY)
    vm = pl.BlockSpec(memory_space=pltpu.VMEM)
    pieces = pl.pallas_call(
        share_kernel,
        out_shape=jax.ShapeDtypeStruct((2, 4, 4, 4, 3, 16, 384), BF16),
        in_specs=[vm],
        out_specs=hbm,
        scratch_shapes=[
            pltpu.VMEM((2, 4, 4, 4, 3, 16, 384), BF16), pltpu.SemaphoreType.DMA, pltpu.SemaphoreType.DMA,
            pltpu.SemaphoreType.DMA((2, 23)),
        ],
        compiler_params=pltpu.CompilerParams(collective_id=3, has_side_effects=True),
    )(blocks)
    return pl.pallas_call(
        assemble_kernel,
        grid=(16,),
        out_shape=jax.ShapeDtypeStruct((D, FF), F32),
        in_specs=[
            pl.BlockSpec((2, 4, 1, 1, 1, 16, 384), lambda b: (0, 0, b // 4, b % 4, 0, 0, 0)),
            pl.BlockSpec((2, 1, 4, 1, 1, 16, 384), lambda b: (0, b % 4, 0, b // 4, 1, 0, 0)),
            pl.BlockSpec((2, 1, 1, 4, 1, 16, 384), lambda b: (0, b // 4, b % 4, 0, 2, 0, 0)),
        ],
        out_specs=pl.BlockSpec((48, FF), lambda b: (b, 0)),
    )(pieces, pieces, pieces)


def on_device(
    tokens, masked, live_images, mask_token, norm_gain, norm_shift, w_first, w_second, layer_scale, rel_table, cotangent
):
    here = masked[0] == 1
    valid = (lax.axis_index("section") < live_images[lax.axis_index("dp")]).astype(F32)

    def pad(array):
        return jnp.pad(array, ((0, ROWS - array.shape[0]), (0, 0)))

    h0 = pad(jnp.where(here[:, None], mask_token[None, :], tokens[0]))
    mask = jnp.broadcast_to(pad(here.astype(F32)[:, None]), (ROWS, 128))
    vec = jnp.concatenate([norm_gain, norm_shift, layer_scale, jnp.zeros((5, D), F32)], axis=0)
    w_all, vecs = gather_all(w_first[0], vec)
    table = jnp.transpose(rel_table, (0, 2, 1)).reshape(2 * HEADS, -1)
    turned = jnp.pad(table[:, : SPAN * SPAN][:, ::-1], ((0, 0), (0, 768 - SPAN * SPAN)))
    corner = jnp.pad(table[:, SPAN * SPAN :], ((0, 0), (0, 125)))
    block_out, tokens_grad, grads, small = layers(
        h0, pad(cotangent[0]), mask, jnp.full((8, 128), valid), w_all, w_second,
        vecs[:, 0], vecs[:, 1], vecs[:, 2], turned, corner,
    )
    first, second, totals = reduce_all(grads, small.reshape(2, 24, D))
    first_grad = share_all(first)
    totals = totals.reshape(48, D)
    count = jnp.sum(live_images).astype(F32) * (SEQ * D)
    rms = jnp.sqrt(jnp.sum(totals[:8], axis=1) / count).reshape(4, 2)
    own = lax.dynamic_slice(totals, (8 + 3 * lax.axis_index("section"), 0), (3, D))
    table_grad = jnp.transpose(totals[24:].reshape(2, HEADS, D)[:, :, :732], (0, 2, 1))
    return (
        block_out[None, :SEQ], tokens_grad[None, :SEQ], first_grad[None], second,
        own[1:2], own[2:3], own[0:1], table_grad, totals[20], rms,
    )


def solution(mesh):
    both = P(("dp", "section"), None, None)
    part = P("section", None)
    return jax.shard_map(
        on_device,
        mesh=mesh,
        in_specs=(both, P(("dp", "section"), None), P(), P(), part, part, P("section", None, None), P(), part, P(), both),
        out_specs=(
            both, both, P("section", None, None), P(None, ("dp", "section"), None), part, part, part, P(), P(), P(),
        ),
        check_vma=False,
    )
```

time: 1540 us -> 402 us (0.26)
  waiting for transfers between devices: 482 us -> 0 us
  Pallas kernels: 0 us -> 378 us
  local copies, waits for them, and re-layouts: 327 us -> 15.4 us
  other arithmetic: 227 us -> 5.32 us
  matrix products: 203 us -> 0 us
  blocking collectives: 139 us -> 0 us
  loops' own time: 85.3 us -> 0 us
  starting transfers between devices: 32 us -> 0 us
  between operations: 30 us -> 2.07 us
    pallas_call x0 -> x5, Pallas kernels: none -> 378 us  [the longest x1 151 us: gather_all(): pl.pallas_call(gather_kernel, out_shape=(jax.ShapeDtypeStruct((4, D, FF),...]
    reduce_scatter x3 -> x0, waiting for transfers between devices: 265 us -> none  [the longest x1 242 us: on_device(): lax.psum_scatter(placed, ('dp', 'section'), scatter_dimension=1, tiled=True)]
    dot_general x78 -> x0, matrix products: 203 us -> none  [the longest x5 33.9 us: expand_bias(): patch_bias = jnp.einsum('ayz,axjh->hyxzj', select, halfway, precision=HIGH)]
    ppermute x12 -> x0, waiting for transfers between devices: 152 us -> none  [from_behind(): return lax.ppermute(array, axis, pairs)]
    reshape x18 -> x2, local copies, waits for them, and re-layouts: 147 us -> 0.02 us  [the longest x1 0.01 us: on_device(): totals[24:].reshape(2, HEADS, D)[:, :, :732]]
    psum x2 -> x0, blocking collectives: 139 us -> none  [the longest x1 77.4 us: on_device(): lax.psum(gain_local.astype(jnp.bfloat16), 'dp').astype(jnp.float32)]
    another operation x21 -> x0, loops' own time: 85.3 us -> none  [the longest x7 52.7 us: on_device(): lax.switch(branch_pick, backwards, resid_in, projected, middle, log_total...]
    another operation x57 -> x0, local copies, waits for them, and re-layouts: 76.8 us -> none
  transfers between devices with their start and end apart: 19 -> 0, of which waited for: 13 -> 0; matrix products, arithmetic and copies ran while one was open for 16% -> 0% of each run, Pallas kernels for 0% -> 0%
where the time goes in v1:
time: 402 us; the launch traced here: 401 us
  Pallas kernels  378 us (94%)
  local copies, waits for them, and re-layouts  15.4 us (4%)
  other arithmetic  5.32 us (1%)
    pallas_call x1, Pallas kernels, gather_all(): pl.pallas_call(gather_kernel, out_shape=(jax.ShapeDtypeStruct((4, D, FF),...  151 us
    pallas_call x1, Pallas kernels, layers(): pl.pallas_call(layers_kernel, out_shape=(jax.ShapeDtypeStruct((ROWS, D),...  101 us
    pallas_call x1, Pallas kernels, reduce_all(): pl.pallas_call(reduce_kernel, out_shape=(jax.ShapeDtypeStruct((4, 3, 16,...  83.9 us
    pallas_call x1, Pallas kernels, share_all(): pl.pallas_call(share_kernel, out_shape=jax.ShapeDtypeStruct((2, 4, 4, 4,...  30.3 us
    pallas_call x1, Pallas kernels, share_all(): pl.pallas_call(assemble_kernel, grid=(16,), out_shape=jax.ShapeDtypeStruc...  11.7 us

profile of v1, /device:TPU:1, one launch (start us, length us, event | category | flops | bytes accessed | tf_op | source)
XLA Modules:
  0.0 400.9 jit_solution(4945093333250699137)
XLA Ops:
  0.6 1.2 dynamic_slice.6
  2.5 0.6 broadcast_in_dim.49.valid
  3.1 0.1 pad.28.clone
  3.2 1.4 maximum_maximum_fusion.vec
  4.6 151.2 %shard_map.204 = (bf16[4,768,3072]{2,1,0:T(8,128)(2,1)}, f32[4,8,768]{2,1,0:T(8,128)}) custom-call(bf16[768,3072]{1,0:T(8,128)(2,1)} %bitcast.27, f32[8,768]{1,0:T(8,128)} %maximum_maximum_fusion.vec), custom_call_target="tpu_custom_call" | custom-call | tf_op jit(solution)/shard_map/pallas_call | solution.py:782
  155.8 0.9 copy.29
  156.8 0.6 slice_bitcast_fusion.3
  157.4 0.7 compare_bitcast_fusion
  158.1 1.1 bitcast_select_fusion
  159.2 0.7 pad.20.h0
  159.9 0.9 copy.32
  160.8 0.5 reverse
  161.3 0.1 slice.73
  161.4 0.7 pad.23.table
  162.0 0.1 slice.61
  162.1 0.6 pad.24.corner
  162.7 0.7 broadcast_in_dim.48.masked
  163.4 1.7 pad.21.cotangent
  165.1 101.1 %shard_map.205 = (bf16[208,768]{1,0:T(8,128)(2,1)}, bf16[208,768]{1,0:T(8,128)(2,1)}, bf16[6,3,2,4,4,4,16,384]{7,6,5,4,3,2,1,0:T(8,128)(2,1)}, f32[48,768]{1,0:T(8,128)}) custom-call(bf16[208,768]{1,0:T(8,128)(2,1)} %pad.20.h0, bf16[208,768]{1,0:T(8,128)(2,1)} %pad.21.cotangent, f32[208,128]{1,0:T(8,128)} %broadcast_in_dim.48.masked, ...), custom_call_target="tpu_custom_call" | custom-call | tf_op jit(solution)/shard_map/pallas_call | solution.py:383
  266.2 83.9 %shard_map.206 = (bf16[4,3,16,384]{3,2,1,0:T(8,128)(2,1)}, f32[2,24,768]{2,1,0:T(8,128)}, f32[2,24,768]{2,1,0:T(8,128)}) custom-call(bf16[6,3,2,4,4,4,16,384]{7,6,5,4,3,2,1,0:T(8,128)(2,1)} %get-tuple-element.23.grads, f32[2,24,768]{2,1,0:T(8,128)} %bitcast.30), custom_call_target="tpu_custom_call" | custom-call | tf_op jit(solution)/shard_map/pallas_call | solution.py:633
  350.1 2.1 slice_reduce_fusion.1
  352.2 0.9 slice_reduce_fusion
  353.1 1.3 reduce_sum.19
  355.0 0.1 sqrt.8
  355.1 0.7 copy.34
  355.8 0.9 slice.53
  356.7 0.7 copy.33
  357.4 30.3 %shard_map.207.first.second.third = bf16[2,4,4,4,3,16,384]{6,5,4,3,2,1,0:T(8,128)(2,1)} custom-call(bf16[4,3,16,384]{3,2,1,0:T(8,128)(2,1)} %get-tuple-element.25.blocks), custom_call_target="tpu_custom_call" | custom-call | tf_op jit(solution)/shard_map/pallas_call | solution.py:865
  387.7 0.0 copy-start
  387.7 11.7 %shard_map.208 = f32[768,3072]{1,0:T(8,128)} custom-call(bf16[2,4,4,4,3,16,384]{6,5,4,3,2,1,0:T(8,128)(2,1)} %shard_map.207.first.second.third, bf16[2,4,4,4,3,16,384]{6,5,4,3,2,1,0:T(8,128)(2,1)} %shard_map.207.first.second.third, bf16[2,4,4,4,3,16,384]{6,5,4,3,2,1,0:T(8,128)(2,1)} %shard_map.207.first.second.third), custom_call_target="tpu_custom_call" | custom-call | tf_op jit(solution)/shard_map/pallas_call | solution.py:876
  399.4 0.9 slice_bitcast_fusion
  400.3 0.7 copy.36
  (11 shorter events, 0.1 us)
Async XLA Ops:
  387.7 11.7 %copy-start = (bf16[208,768]{1,0:T(8,128)(2,1)S(1)}, bf16[208,768]{1,0:T(8,128)(2,1)}, u32[]{:S(2)}) copy-start(bf16[208,768]{1,0:T(8,128)(2,1)} %get-tuple-element.21) | copy-start | bytes 958468
  387.7 11.7 %copy-start.1 = (bf16[208,768]{1,0:T(8,128)(2,1)S(1)}, bf16[208,768]{1,0:T(8,128)(2,1)}, u32[]{:S(2)}) copy-start(bf16[208,768]{1,0:T(8,128)(2,1)} %get-tuple-element.22) | copy-start | bytes 958468
  387.7 12.6 %copy-start.2 = (f32[2,24,768]{2,1,0:T(8,128)S(1)}, f32[2,24,768]{2,1,0:T(8,128)}, u32[]{:S(2)}) copy-start(f32[2,24,768]{2,1,0:T(8,128)} %get-tuple-element.72) | copy-start | bytes 442372

commit v2 on v1

v2 whole, which is shorter than its diff:
```python
import functools
import math

import jax
import jax.numpy as jnp
import numpy as np
from jax import lax
from jax.experimental import pallas as pl
from jax.experimental.pallas import tpu as pltpu
from jax.sharding import PartitionSpec as P

SEQ, ROWS, KEYS = 197, 208, 256
D, FF, HEADS, GRID = 768, 3072, 12, 14
SPAN = 2 * GRID - 1
EPSILON = 1e-06
INV_ROOT = 0.125
INV_ROOT_TWO_PI = 0.3989422804014327
F32, BF16 = jnp.float32, jnp.bfloat16
HALF = (3, 4, 4, 4, 16, 384)


def mm(a, b):
    return lax.dot_general(a, b, (((1,), (0,)), ((), ())), preferred_element_type=F32)


def mm_nt(a, b):
    return lax.dot_general(a, b, (((1,), (1,)), ((), ())), preferred_element_type=F32)


def mm_tn(a, b):
    return lax.dot_general(a, b, (((0,), (0,)), ((), ())), preferred_element_type=F32)


def lanes(start, size):
    return pl.ds(pl.multiple_of(start, 128), size)


def token_offsets():
    patch = np.arange(SEQ - 1)
    return (patch // GRID) * SPAN + patch % GRID


def selectors():
    forward = np.zeros((384, KEYS), np.float32)
    backward = np.zeros((KEYS, 384), np.float32)
    offsets = token_offsets()
    forward[offsets, np.arange(1, SEQ)] = 1.0
    backward[np.arange(1, SEQ), offsets[-1] - offsets] = 1.0
    return jnp.asarray(forward, BF16), jnp.asarray(backward, BF16)


def centre(h):
    average = jnp.mean(h, axis=-1, keepdims=True)
    centred = h - average
    inv_std = lax.rsqrt(jnp.mean(centred * centred, axis=-1, keepdims=True) + EPSILON)
    return centred * inv_std, inv_std


def gelu_pair(u):
    size = jnp.abs(u)
    t = 1.0 / (1.0 + 0.23164189 * size)
    bell = jnp.exp(-0.5 * u * u)
    poly = t * (
        0.127414796
        + t * (-0.142248368 + t * (0.7107068705 + t * (-0.7265760135 + t * 0.5307027145)))
    )
    tail = poly * bell
    phi = jnp.where(u >= 0.0, 1.0 - tail, tail)
    return u * phi, phi + u * bell * INV_ROOT_TWO_PI


def half_mask(rows, parity):
    lane = lax.broadcasted_iota(jnp.int32, (rows, 128), 1)
    return (lane < 64) if parity == 0 else (lane >= 64)


def keep_half(block, parity):
    return jnp.where(half_mask(block.shape[0], parity), block, jnp.zeros_like(block))


class Body:
    def __init__(self, **refs):
        self.__dict__.update(refs)

    def expand_bias(self, layer):
        def head(index, _):
            base = jnp.broadcast_to(self.table[pl.ds(layer * HEADS + index, 1), :], (16, 768))
            base = pltpu.roll(base, 404, 1, stride=1, stride_axis=0)
            for yi in range(GRID):
                turned = pltpu.roll(base, SPAN * yi, 1) if yi else base
                self.fold[1 + GRID * yi : 1 + GRID * (yi + 1), :384] = turned[:GRID, :384]
            spread = self.fold[:, :384]
            high = spread.astype(BF16)
            low = (spread - high.astype(F32)).astype(BF16)
            select = self.select_forward[...]
            grid = mm(high, select) + mm(low, select)
            row = lax.broadcasted_iota(jnp.int32, (ROWS, KEYS), 0)
            column = lax.broadcasted_iota(jnp.int32, (ROWS, KEYS), 1)
            corner = self.corner[pl.ds(layer * HEADS + index, 1), :]
            grid = jnp.where(row == 0, corner[:, 0:1], grid)
            grid = jnp.where(column == 0, corner[:, 1:2], grid)
            grid = jnp.where((row == 0) & (column == 0), corner[:, 2:3], grid)
            self.bias[index] = jnp.where(column >= SEQ, -1e30, grid)
            return 0

        lax.fori_loop(0, HEADS, head, 0)

    def normed(self, s):
        scaled, _ = centre(self.h[s].astype(F32))
        gain = self.vecs[s, 0:1, :]
        shift = self.vecs[s, 1:2, :]
        self.n[0] = (scaled * gain + shift).astype(BF16)

    def finish(self, s, left, right_of):
        real = (lax.broadcasted_iota(jnp.int32, (ROWS, 1), 0) < SEQ).astype(F32) * self.valid

        def block(j, _):
            columns = lanes(j * 256, 256)
            projected = mm(left[...], right_of(columns))
            branch = self.vecs[s, 2:3, columns] * projected
            result = self.h[s, :, columns].astype(F32) + branch
            self.p[s, :, columns] = projected.astype(BF16)
            self.small[2 * s : 2 * s + 1, columns] = jnp.sum(branch * branch * real, axis=0, keepdims=True)
            self.small[2 * s + 1 : 2 * s + 2, columns] = jnp.sum(result * result * real, axis=0, keepdims=True)
            if s < 3:
                self.h[s + 1, :, columns] = result.astype(BF16)
            else:
                self.block_out[0, :, columns] = (result[:SEQ] * self.valid).astype(BF16)
            return 0

        lax.fori_loop(0, 3, block, 0)

    def attend_forward(self, s):
        layer = s // 2
        self.normed(s)

        def project(j, _):
            columns = lanes(j * 256, 256)
            self.qkv[layer, :ROWS, columns] = mm(self.n[0], self.w[s, :, columns]).astype(BF16)
            return 0

        lax.fori_loop(0, 9, project, 0)
        self.qkv[layer, ROWS:, :] = jnp.zeros((KEYS - ROWS, 2304), BF16)

        def pair(j, _):
            q = self.qkv[layer, :ROWS, lanes(j * 128, 128)]
            k = self.qkv[layer, :, lanes(768 + j * 128, 128)]
            v = self.qkv[layer, :, lanes(1536 + j * 128, 128)]
            mixed = jnp.zeros((ROWS, 128), F32)
            for parity in range(2):
                scores = mm_nt(keep_half(q, parity), k) * INV_ROOT + self.bias[2 * j + parity]
                peak = jnp.max(scores, axis=-1, keepdims=True)
                exps = jnp.exp(scores - peak)
                total = jnp.sum(exps, axis=-1, keepdims=True)
                probs = (exps * (1.0 / total)).astype(BF16)
                self.probs[layer, 2 * j + parity] = probs
                mixed = mixed + mm(probs, keep_half(v, parity))
            self.o[layer, :, lanes(j * 128, 128)] = mixed.astype(BF16)
            return 0

        lax.fori_loop(0, HEADS // 2, pair, 0)
        self.finish(s, self.o.at[layer], lambda c: self.w[s, :, pl.ds(pl.multiple_of(2304 + c.start, 128), 256)])

    def dense_forward(self, s):
        layer = s // 2
        self.normed(s)

        def up(j, _):
            columns = lanes(j * 256, 256)
            u = mm(self.n[0], self.w[s, :, columns])
            act, slope = gelu_pair(u)
            self.a[layer, :, columns] = act.astype(BF16)
            self.slope[layer, :, columns] = slope.astype(BF16)
            return 0

        lax.fori_loop(0, 12, up, 0)
        self.finish(s, self.a.at[layer], lambda c: self.w2[:, c])

    def enter(self, s):
        g = self.g[...].astype(F32)
        row = 8 + 3 * s
        self.small[row : row + 1, :] = jnp.sum(g * self.p[s].astype(F32), axis=0, keepdims=True)
        dp = (g * self.vecs[s, 2:3, :]).astype(BF16)
        self.dp[...] = dp
        self.normed(s)
        if s % 2 == 0:
            self.n[1] = self.o[s // 2]
            self.du[:, 2304:] = dp

    def leave(self, s):
        width = 2304 if s % 2 == 0 else FF

        def block(j, _):
            rows = pl.ds(pl.multiple_of(j * 256, 256), 256)
            self.bias[j] = mm_nt(self.du[:, :width], self.w[s, rows, :width])
            return 0

        lax.fori_loop(0, 3, block, 0)
        scaled, inv_std = centre(self.h[s].astype(F32))
        dn = jnp.concatenate([self.bias[0], self.bias[1], self.bias[2]], axis=1)
        row = 8 + 3 * s
        self.small[row + 1 : row + 2, :] = jnp.sum(dn * scaled, axis=0, keepdims=True)
        self.small[row + 2 : row + 3, :] = jnp.sum(dn, axis=0, keepdims=True)
        e = dn * self.vecs[s, 0:1, :]
        mean_e = jnp.mean(e, axis=-1, keepdims=True)
        mean_ex = jnp.mean(e * scaled, axis=-1, keepdims=True)
        g = self.g[...].astype(F32) + inv_std * (e - mean_e - scaled * mean_ex)
        self.g[...] = g.astype(BF16)

    def put(self, k, mine, route, a1, a2, a3, piece):
        if mine:
            pair = self.pair.at[k % 2, route, a1, a2, a3]
            pair[...] = (piece + pair[...].astype(F32)).astype(BF16)
        else:
            self.stage[k % 2, route, a1, a2, a3] = piece.astype(BF16)

    def first_half(self, k, mine):
        half = self.core if mine else 1 - self.core

        def block(a3, _):
            j = half * 4 + a3
            left = jnp.where(j >= self.switch, 1, 0)
            grad = mm_tn(self.n[left], self.du[:, lanes(j * 384, 384)])
            for rb in range(16):
                for route in range(3):
                    top = rb * 48 + route * 16
                    self.put(k, mine, route, rb // 4, rb % 4, a3, grad[top : top + 16, :])
            return 0

        lax.fori_loop(0, 4, block, 0)

    def second_half(self, k, mine, layer):
        half = self.core if mine else 1 - self.core

        def block(q, _):
            z, x_high = q // 2, q % 2
            grad = mm_tn(self.a[layer, :, lanes(q * 384, 384)], self.dp[:, lanes(half * 384, 384)])
            for x_low in range(2):
                x = 2 * x_high + x_low
                for y in range(4):
                    top = x_low * 192 + y * 24
                    part = jnp.concatenate([grad[top : top + 24], grad[top + 96 : top + 120]], axis=0)
                    self.put(k, mine, 0, x, y, z, part[0:16])
                    self.put(k, mine, 1, y, z, x, part[16:32])
                    self.put(k, mine, 2, z, x, y, part[32:48])
            return 0

        lax.fori_loop(0, 8, block, 0)

    def down(self, s):
        layer = s // 2

        def block(j, _):
            columns = lanes(j * 256, 256)
            rows = pl.ds(pl.multiple_of(j * 256, 256), 256)
            da = mm_nt(self.dp[...], self.w2[rows, :])
            self.du[:, columns] = (da * self.slope[layer, :, columns].astype(F32)).astype(BF16)
            return 0

        lax.fori_loop(0, 12, block, 0)

    def back_out(self, s):
        def block(j, _):
            rows = pl.ds(pl.multiple_of(j * 256, 256), 256)
            self.do[:, lanes(j * 256, 256)] = mm_nt(self.dp[...], self.w[s, rows, 2304:]).astype(BF16)
            return 0

        lax.fori_loop(0, 3, block, 0)

    def pairs(self, s, lo, hi):
        layer = s // 2

        def pair(j, _):
            q = self.qkv[layer, :ROWS, lanes(j * 128, 128)]
            k = self.qkv[layer, :, lanes(768 + j * 128, 128)]
            v = self.qkv[layer, :, lanes(1536 + j * 128, 128)]
            do = self.do[:, lanes(j * 128, 128)]
            dq = jnp.zeros((ROWS, 128), F32)
            dk = jnp.zeros((KEYS, 128), F32)
            dv = jnp.zeros((KEYS, 128), F32)
            for parity in range(2):
                do_half = keep_half(do, parity)
                probs = self.probs[layer, 2 * j + parity]
                wide = probs.astype(F32)
                d_probs = mm_nt(do_half, v)
                inner = jnp.sum(d_probs * wide, axis=-1, keepdims=True)
                d_scores = (wide * (d_probs - inner)).astype(BF16)
                dv = dv + mm_tn(probs, do_half)
                dq = dq + mm(d_scores, keep_half(k, parity))
                dk = dk + mm_tn(d_scores, keep_half(q, parity))
                self.fold_bias(layer, 2 * j + parity, d_scores)
            self.du[:, lanes(j * 128, 128)] = (dq * INV_ROOT).astype(BF16)
            self.du[:, lanes(768 + j * 128, 128)] = (dk[:ROWS] * INV_ROOT).astype(BF16)
            self.du[:, lanes(1536 + j * 128, 128)] = dv[:ROWS].astype(BF16)
            return 0

        lax.fori_loop(lo, hi, pair, 0)

    def fold_bias(self, layer, head, d_scores):
        self.fold[:, :384] = mm(d_scores, self.select_backward[...])
        total = self.fold[1:17, :]
        for yi in range(1, GRID):
            total = total + pltpu.roll(self.fold[1 + GRID * yi : 17 + GRID * yi, :], SPAN * yi, 1)
        row = lax.broadcasted_iota(jnp.int32, (16, 768), 0)
        total = jnp.where(row < GRID, total, 0.0)
        total = pltpu.roll(total, 0, 1, stride=1, stride_axis=0)
        total = jnp.sum(total, axis=0, keepdims=True)
        wide = d_scores.astype(F32)
        corner = wide[0:1, 0:1]
        top = jnp.sum(wide[0:1, :], axis=1, keepdims=True) - corner
        side = jnp.sum(wide[:, 0:1], axis=0, keepdims=True) - corner
        lane = lax.broadcasted_iota(jnp.int32, (1, 768), 1)
        total = jnp.where(lane == 729, top, total)
        total = jnp.where(lane == 730, side, total)
        total = jnp.where(lane == 731, corner, total)
        self.small[pl.ds(24 + layer * HEADS + head, 1), :] = total


MESH = pl.DeviceIdType.MESH
AXES = ("x", "y", "z")
ROUTES = (("x", "y", "z"), ("y", "z", "x"), ("z", "x", "y"))
ORDER = (5, 3, 2, 4, 1, 0)


class Place:
    def __init__(self):
        dp = lax.axis_index("dp")
        self.at = {"z": dp // 8, "x": (dp // 2) % 4, "c": dp % 2, "y": lax.axis_index("section")}

    def go(self, axis, step):
        at = dict(self.at)
        at[axis] = (at[axis] + step) % (2 if axis == "c" else 4)
        return ((at["z"] * 4 + at["x"]) * 2 + at["c"], at["y"])

    def index(self, axis, step=0):
        return (self.at[axis] + step) % 4


def meet(place):
    barrier = pltpu.get_barrier_semaphore()
    count = 0
    for axis in AXES:
        for step in (1, 2, 3):
            pl.semaphore_signal(barrier, inc=1, device_id=place.go(axis, step), device_id_type=MESH)
            count += 1
    pl.semaphore_signal(barrier, inc=1, device_id=place.go("c", 1), device_id_type=MESH)
    pl.semaphore_wait(barrier, count + 1)


class Reduce:
    def __init__(self, place, **refs):
        self.place = place
        self.__dict__.update(refs)
        self.flying = {}

    def send(self, key, src, dst, number, device):
        k = key[1]
        copy = pltpu.make_async_remote_copy(
            src_ref=src, dst_ref=dst, send_sem=self.sems.at[0, k, number], recv_sem=self.sems.at[1, k, number],
            device_id=device, device_id_type=MESH,
        )
        copy.start()
        self.flying[key] = copy

    def sent(self, k, names):
        for name in names:
            for r in range(3):
                self.flying[(name, k, r)].wait_send()

    def reuse_stage(self, k):
        if k >= 2:
            self.sent(k - 2, ("c",))

    def swap(self, k):
        if k >= 2:
            pl.semaphore_wait(self.pair_credit, 1)
        for r in range(3):
            self.send(("c", k, r), self.stage.at[k % 2, r], self.pair.at[k % 2, r], r, self.place.go("c", 1))

    def swapped(self, k):
        for r in range(3):
            self.flying[("c", k, r)].wait_recv()

    def first(self, k):
        place = self.place
        for r, (axis, _, _) in enumerate(ROUTES):
            own, far = self.pair.at[k % 2, r], self.far.at[k % 2, r]
            across, ahead, behind = place.index(axis, 2), place.index(axis, 1), place.index(axis, 3)
            up, down = place.go(axis, 1), place.go(axis, 3)
            base = 3 + 6 * r
            if k >= 2:
                pl.semaphore_wait(self.far_credit.at[r, 0], 1)
                pl.semaphore_wait(self.far_credit.at[r, 1], 1)
            self.send(("fa", k, r), own.at[across, 0:2], far.at[0], base, up)
            self.send(("fb", k, r), own.at[across, 2:4], far.at[1], base + 1, down)
            self.send(("db", k, r), own.at[ahead, 2:4], far.at[2], base + 2, up)
            self.send(("da", k, r), own.at[behind, 0:2], far.at[3], base + 3, down)

    def merge(self, k):
        place = self.place
        for r, (axis, _, _) in enumerate(ROUTES):
            own, far = self.pair.at[k % 2, r], self.far.at[k % 2, r]
            ahead, behind = place.index(axis, 1), place.index(axis, 3)
            base = 3 + 6 * r
            self.flying[("fa", k, r)].wait_recv()
            far[0] = (far[0].astype(F32) + own[ahead, 0:2].astype(F32)).astype(BF16)
            self.send(("ma", k, r), far.at[0], far.at[4], base + 4, place.go(axis, 1))
            self.flying[("fb", k, r)].wait_recv()
            far[1] = (far[1].astype(F32) + own[behind, 2:4].astype(F32)).astype(BF16)
            self.send(("mb", k, r), far.at[1], far.at[5], base + 5, place.go(axis, 3))

    def second(self, k):
        place = self.place
        for r, (axis, nxt, _) in enumerate(ROUTES):
            for name in ("db", "da", "ma", "mb"):
                self.flying[(name, k, r)].wait_recv()
            own, far = self.pair.at[k % 2, r], self.far.at[k % 2, r]
            me = place.index(axis)
            low = own[me, 0:2].astype(F32) + far[4].astype(F32) + far[3].astype(F32)
            high = own[me, 2:4].astype(F32) + far[2].astype(F32) + far[5].astype(F32)
            line, line_in = self.line.at[k % 2, r], self.line_in.at[k, r]
            line[0:2] = low.astype(BF16)
            line[2:4] = high.astype(BF16)
            for step in (1, 2, 3):
                self.send(
                    (("s", step), k, r), line.at[place.index(nxt, step)], line_in.at[step - 1],
                    21 + 3 * r + step - 1, place.go(nxt, step),
                )
        self.sent(k, ("fa", "fb", "db", "da", "ma", "mb"))
        if k + 2 < 6:
            pl.semaphore_signal(self.pair_credit, inc=1, device_id=place.go("c", 1), device_id_type=MESH)
            for r, (axis, _, _) in enumerate(ROUTES):
                pl.semaphore_signal(self.far_credit.at[r, 0], inc=1, device_id=place.go(axis, 1), device_id_type=MESH)
                pl.semaphore_signal(self.far_credit.at[r, 1], inc=1, device_id=place.go(axis, 3), device_id_type=MESH)

    def third(self, k):
        place = self.place
        for r, (_, axis, nxt) in enumerate(ROUTES):
            line, line_in, spot, spot_in = self.line.at[k % 2, r], self.line_in.at[k, r], self.spot.at[k % 2, r], self.spot_in.at[k, r]
            total = line[place.index(axis)].astype(F32)
            for step in (1, 2, 3):
                self.flying[(("s", step), k, r)].wait_recv()
                total = total + line_in[step - 1].astype(F32)
            spot[...] = total.astype(BF16)
            for step in (1, 2, 3):
                self.send(
                    (("t", step), k, r), spot.at[place.index(nxt, step)], spot_in.at[step - 1],
                    30 + 3 * r + step - 1, place.go(nxt, step),
                )
        self.sent(k, (("s", 1), ("s", 2), ("s", 3)))

    def close(self, k):
        place, tensor = self.place, ORDER[k]
        for r, (_, _, axis) in enumerate(ROUTES):
            spot, spot_in = self.spot.at[k % 2, r], self.spot_in.at[k, r]
            total = spot[place.index(axis)].astype(F32)
            for step in (1, 2, 3):
                self.flying[(("t", step), k, r)].wait_recv()
                total = total + spot_in[step - 1].astype(F32)
            if tensor < 4:
                self.first_out[tensor, r] = total.astype(BF16)
            else:
                rows = self.rows.at[tensor - 4]
                if r == 0:
                    rows[0, 0:16] = total
                elif r == 1:
                    rows[0, 16:24] = total[0:8]
                    rows[1, 0:8] = total[8:16]
                else:
                    rows[1, 8:24] = total
        self.sent(k, (("t", 1), ("t", 2), ("t", 3)))
        if tensor >= 4:
            layer, me = tensor - 4, place.at["c"]
            self.send(("r", k, 0), self.rows.at[layer, 1 - me], self.rows_in.at[layer], 39, place.go("c", 1))

    def finish(self):
        me = self.place.at["c"]
        for k, tensor in enumerate(ORDER):
            if tensor >= 4:
                self.flying[("r", k, 0)].wait()
                layer = tensor - 4
                self.second_out[layer, :, lanes(me * 384, 384)] = self.rows[layer, me]
                self.second_out[layer, :, lanes((1 - me) * 384, 384)] = self.rows_in[layer]
        for k in (4, 5):
            self.sent(k, ("c",))


class Totals:
    def __init__(self, place, part, bufs, sems):
        self.place, self.part, self.bufs, self.sems = place, part, bufs, sems
        self.copies = []

    def send(self, src, dst, number, device):
        copy = pltpu.make_async_remote_copy(
            src_ref=src, dst_ref=dst, send_sem=self.sems.at[0, number], recv_sem=self.sems.at[1, number],
            device_id=device, device_id_type=MESH,
        )
        copy.start()
        self.copies.append(copy)
        return copy

    @staticmethod
    def half(core):
        return pl.ds(pl.multiple_of(core * 24, 8), 24)

    def start(self, small):
        me = self.place.at["c"]
        self.small = small
        self.now = [self.send(small.at[self.half(1 - me)], self.bufs.at[0, 0], 0, self.place.go("c", 1))]

    def step(self, number):
        place, me = self.place, self.place.at["c"]
        for copy in self.now:
            copy.wait_recv()
        if number == 0:
            self.part[...] = self.small[self.half(me), :] + self.bufs[0, 0]
        else:
            axis = AXES[number - 1]
            self.bufs[number, place.at[axis]] = self.part[...]
            self.part[...] = (self.bufs[number, 0] + self.bufs[number, 1]) + (self.bufs[number, 2] + self.bufs[number, 3])
        if number < 3:
            axis = AXES[number]
            self.now = [
                self.send(self.part, self.bufs.at[number + 1, place.at[axis]], 1 + 3 * number + step - 1, place.go(axis, step))
                for step in (1, 2, 3)
            ]
            for copy in self.now:
                copy.wait_send()
        else:
            self.now = [self.send(self.part, self.bufs.at[0, 1], 10, place.go("c", 1))]

    def close(self, out):
        me = self.place.at["c"]
        for copy in self.now:
            copy.wait_recv()
        out[self.half(me), :] = self.part[...]
        out[self.half(1 - me), :] = self.bufs[0, 1]
        self.copies[0].wait_send()
        self.copies[-1].wait_send()


class Spread:
    def __init__(self, place, sems):
        self.place, self.sems = place, sems
        self.sent = []

    def send(self, number, src, dst, device):
        copy = pltpu.make_async_remote_copy(
            src_ref=src, dst_ref=dst, send_sem=self.sems.at[0, number], recv_sem=self.sems.at[1, number],
            device_id=device, device_id_type=MESH,
        )
        copy.start()
        self.sent.append(copy)

    def wait(self, number, ref):
        pltpu.make_async_remote_copy(
            src_ref=ref, dst_ref=ref, send_sem=self.sems.at[0, number], recv_sem=self.sems.at[1, number],
            device_id=self.place.go("c", 1), device_id_type=MESH,
        ).wait_recv()

    def drain(self):
        for copy in self.sent:
            copy.wait_send()


GATHER_MESSAGES = 99


class Gather(Spread):
    def __init__(self, place, source, full, sems):
        super().__init__(place, sems)
        self.source, self.full = source, full

    def rows(self, route, step, sub=None):
        top = (0 if route == "x" else 384) + self.place.index(route, step) * 96 + self.place.at["c"] * 48
        if sub is None:
            return pl.ds(pl.multiple_of(top, 16), 48)
        return pl.ds(pl.multiple_of(top + 16 * sub, 16), 16)

    def ref(self, rel, route, step, sub=None):
        return self.full.at[self.place.index("y", rel), self.rows(route, step, sub)]

    @staticmethod
    def along_y(rel, route, sub):
        return 3 * (2 * (rel - 1) + (route == "z")) + sub

    @staticmethod
    def in_plane(rel, route, kind, sub):
        return 18 + 9 * (2 * (rel - 1) + (route == "z")) + 3 * kind + sub

    @staticmethod
    def across(rel, route, step):
        return 72 + 4 * (2 * (rel - 1) + (route == "z")) + step

    def begin(self, up, down):
        for sub in range(3):
            for route, step in ((up, 1), (down, 3)):
                mine = self.source.at[self.rows(route, 0, sub)]
                self.send(self.along_y(4 - step, route, sub), mine, self.ref(0, route, 0, sub), self.place.go("y", step))

    def arrive(self, *pieces):
        for sub in range(3):
            for rel, route in pieces:
                piece = self.ref(rel, route, 0, sub)
                self.wait(self.along_y(rel, route, sub), piece)
                if (rel, route) == (3, "x"):
                    self.send(self.along_y(2, route, sub), piece, piece, self.place.go("y", 1))
                if (rel, route) == (1, "z"):
                    self.send(self.along_y(2, route, sub), piece, piece, self.place.go("y", 3))
                for kind, step in ((0, 1), (1, 3)):
                    self.send(self.in_plane(rel, route, kind, sub), piece, piece, self.place.go(route, step))
        for rel, route in pieces:
            piece = self.ref(rel, route, 0)
            self.send(self.across(rel, route, 0), piece, piece, self.place.go("c", 1))

    def turn(self, *pieces):
        place = self.place
        clockwise = 1 - 2 * place.at["c"]
        for sub, way in ((0, 1), (1, clockwise), (2, -1)):
            for rel, route in pieces:
                for kind, step in ((0, 3), (1, 1)):
                    self.wait(self.in_plane(rel, route, kind, sub), self.ref(rel, route, step, sub))
                piece = self.ref(rel, route, 4 - way, sub)
                self.send(self.in_plane(rel, route, 2, sub), piece, piece, place.go(route, 4 + way))
        for rel, route in pieces:
            for step in (3, 1):
                piece = self.ref(rel, route, step)
                self.send(self.across(rel, route, step), piece, piece, place.go("c", 1))

    def end(self, *pieces):
        for rel, route in pieces:
            for sub in range(3):
                self.wait(self.in_plane(rel, route, 2, sub), self.ref(rel, route, 2, sub))
            piece = self.ref(rel, route, 2)
            self.send(self.across(rel, route, 2), piece, piece, self.place.go("c", 1))

    def settle(self, rel):
        other = 1 - self.place.at["c"]
        for route in ("x", "z"):
            for step in range(4):
                top = (0 if route == "x" else 384) + self.place.index(route, step) * 96 + other * 48
                self.wait(self.across(rel, route, step), self.full.at[self.place.index("y", rel), pl.ds(pl.multiple_of(top, 16), 48)])


def layers_kernel(
    tokens, masked, cotangent, live, mask_token, norm_gain, norm_shift, layer_scale, w_own, w2_hbm,
    table, corner, select_f, select_b,
    block_out, tokens_grad, first_out, second_out, totals,
    w, w2, h, qkv, probs, o, a, slope, p, n, bias, fold, du, dp, do, g, vec, vecs, small,
    stage, pair, far, line, line_in, spot, spot_in, rows, rows_in, part, bufs,
    load_sem, w2_sem, gather_sems, sems, small_sems, pair_credit, far_credit,
):
    place = Place()
    vec[0:1] = norm_gain[...]
    vec[1:2] = norm_shift[...]
    vec[2:3] = layer_scale[...]
    vec[3:8] = jnp.zeros((5, D), F32)
    meet(place)
    y = place.at["y"]
    own = pltpu.make_async_copy(w_own.at[0], w.at[y], load_sem)
    own.start()
    w2_load = pltpu.make_async_copy(w2_hbm.at[0], w2, w2_sem)
    w2_load.start()
    gather = Gather(place, w_own.at[0], w, gather_sems)
    gather.begin("x", "z")
    vecs[y] = vec[...]
    for step in (1, 2, 3):
        gather.send(95 + step, vec, vecs.at[y], place.go("y", step))
    valid = jnp.where(y < live[lax.axis_index("dp")], 1.0, 0.0)
    body = Body(
        valid=valid, core=place.at["c"], vecs=vecs, table=table, corner=corner,
        select_forward=select_f, select_backward=select_b, block_out=block_out, small=small,
        w=w, w2=w2, h=h, qkv=qkv, probs=probs, o=o, a=a, slope=slope, p=p, n=n, bias=bias,
        fold=fold, du=du, dp=dp, do=do, g=g, stage=stage, pair=pair,
    )
    reduce = Reduce(
        place, stage=stage, pair=pair, far=far, line=line, line_in=line_in, spot=spot, spot_in=spot_in,
        rows=rows, rows_in=rows_in, first_out=first_out, second_out=second_out, sems=sems,
        pair_credit=pair_credit, far_credit=far_credit,
    )
    sums = Totals(place, part, bufs, small_sems)

    gather.arrive((3, "x"), (1, "z"))
    gather.begin("z", "x")
    fold[...] = jnp.zeros_like(fold)
    square = (ROWS, KEYS)
    diagonal = lax.broadcasted_iota(jnp.int32, square, 0) == lax.broadcasted_iota(jnp.int32, square, 1)
    flags = jnp.concatenate([masked[...].astype(F32), jnp.zeros((1, KEYS - SEQ), F32)], axis=1)
    here = jnp.sum(jnp.where(diagonal, flags, 0.0), axis=1, keepdims=True)
    h[0, 192:] = jnp.zeros((16, D), BF16)
    start = tokens[0].astype(F32)
    h[0, :SEQ] = (start + here[:SEQ] * (mask_token[...].astype(F32) - start)).astype(BF16)
    g[192:] = jnp.zeros((16, D), BF16)
    g[:SEQ] = (cotangent[0].astype(F32) * valid).astype(BF16)
    body.expand_bias(0)
    gather.arrive((2, "x"), (2, "z"))
    gather.turn((3, "x"), (1, "z"))
    gather.arrive((1, "x"), (3, "z"))
    gather.turn((2, "x"), (2, "z"))
    gather.end((3, "x"), (1, "z"))
    gather.turn((1, "x"), (3, "z"))
    gather.end((2, "x"), (2, "z"), (1, "x"), (3, "z"))
    for rel in (3, 1, 2):
        gather.settle(rel)
    for step in (1, 2, 3):
        gather.wait(95 + step, vecs.at[place.index("y", 4 - step)])
    own.wait()
    body.attend_forward(0)
    w2_load.wait()
    body.dense_forward(1)
    w2_load = pltpu.make_async_copy(w2_hbm.at[1], w2, w2_sem)
    w2_load.start()
    body.expand_bias(1)
    body.attend_forward(2)
    w2_load.wait()
    body.dense_forward(3)
    gather.drain()

    body.switch = 8
    body.enter(3)
    body.second_half(0, False, 1)
    reduce.swap(0)
    body.down(3)
    w2_load = pltpu.make_async_copy(w2_hbm.at[0], w2, w2_sem)
    w2_load.start()
    reduce.swapped(0)
    body.second_half(0, True, 1)
    reduce.first(0)
    body.first_half(1, False)
    reduce.swap(1)
    body.leave(3)
    reduce.merge(0)
    reduce.swapped(1)
    body.first_half(1, True)
    reduce.first(1)
    body.switch = 6
    body.enter(2)
    body.back_out(2)
    reduce.second(0)
    body.pairs(2, 0, 3)
    reduce.merge(1)
    body.pairs(2, 3, 6)
    reduce.third(0)
    reduce.reuse_stage(2)
    body.first_half(2, False)
    reduce.swap(2)
    body.leave(2)
    reduce.second(1)
    reduce.swapped(2)
    body.first_half(2, True)
    reduce.first(2)
    reduce.close(0)
    body.switch = 8
    body.enter(1)
    reduce.reuse_stage(3)
    body.second_half(3, False, 0)
    reduce.swap(3)
    reduce.third(1)
    w2_load.wait()
    body.down(1)
    reduce.merge(2)
    reduce.swapped(3)
    body.second_half(3, True, 0)
    reduce.first(3)
    reduce.reuse_stage(4)
    body.first_half(4, False)
    reduce.second(2)
    reduce.swap(4)
    reduce.close(1)
    body.leave(1)
    reduce.merge(3)
    reduce.swapped(4)
    body.first_half(4, True)
    reduce.first(4)
    body.switch = 6
    body.enter(0)
    body.back_out(0)
    reduce.third(2)
    reduce.second(3)
    body.pairs(0, 0, 3)
    reduce.merge(4)
    reduce.close(2)
    body.pairs(0, 3, 6)
    reduce.third(3)
    reduce.reuse_stage(5)
    body.first_half(5, False)
    reduce.swap(5)
    body.leave(0)
    grad = g[...].astype(F32)
    tokens_grad[0] = (grad * (1.0 - here)).astype(BF16)[:SEQ]
    small[20:21, :] = jnp.sum(grad * here, axis=0, keepdims=True)
    small[21:24, :] = jnp.zeros((3, D), F32)
    sums.start(small)
    reduce.second(4)
    reduce.swapped(5)
    body.first_half(5, True)
    reduce.first(5)
    reduce.close(3)
    sums.step(0)
    reduce.third(4)
    reduce.merge(5)
    sums.step(1)
    reduce.close(4)
    reduce.second(5)
    sums.step(2)
    reduce.third(5)
    sums.step(3)
    reduce.close(5)
    sums.close(totals)
    reduce.finish()


def layers(tokens, masked, cotangent, live, mask_token, norm_gain, norm_shift, layer_scale, w_own, w2, table, corner):
    select_f, select_b = selectors()
    vm = pl.BlockSpec(memory_space=pltpu.VMEM)
    hbm = pl.BlockSpec(memory_space=pl.ANY)
    sm = pl.BlockSpec(memory_space=pltpu.SMEM)
    V, DMA, REGULAR = pltpu.VMEM, pltpu.SemaphoreType.DMA, pltpu.SemaphoreType.REGULAR
    return pl.pallas_call(
        layers_kernel,
        out_shape=(
            jax.ShapeDtypeStruct((1, SEQ, D), BF16),
            jax.ShapeDtypeStruct((1, SEQ, D), BF16),
            jax.ShapeDtypeStruct((4, 3, 16, 384), BF16),
            jax.ShapeDtypeStruct((2, 24, D), F32),
            jax.ShapeDtypeStruct((48, D), F32),
        ),
        in_specs=[vm, vm, vm, sm, vm, vm, vm, vm, hbm, hbm, vm, vm, vm, vm],
        out_specs=(vm,) * 5,
        scratch_shapes=[
            V((4, D, FF), BF16), V((FF, D), BF16), V((4, ROWS, D), BF16), V((2, KEYS, 2304), BF16),
            V((2, HEADS, ROWS, KEYS), BF16), V((2, ROWS, D), BF16), V((2, ROWS, FF), BF16), V((2, ROWS, FF), BF16),
            V((4, ROWS, D), BF16), V((2, ROWS, D), BF16), V((HEADS, ROWS, KEYS), F32),
            V((ROWS, D), F32), V((ROWS, FF), BF16), V((ROWS, D), BF16), V((ROWS, D), BF16), V((ROWS, D), BF16),
            V((8, D), F32), V((4, 8, D), F32), V((48, D), F32),
            V((2,) + HALF, BF16), V((2,) + HALF, BF16), V((2, 3, 6, 2, 4, 16, 384), BF16),
            V((2, 3, 4, 4, 16, 384), BF16), V((6, 3, 3, 4, 16, 384), BF16),
            V((2, 3, 4, 16, 384), BF16), V((6, 3, 3, 16, 384), BF16),
            V((2, 2, 24, 384), F32), V((2, 24, 384), F32), V((24, D), F32), V((4, 4, 24, D), F32),
            DMA, DMA, DMA((2, GATHER_MESSAGES)), DMA((2, 6, 40)), DMA((2, 11)), REGULAR, REGULAR((3, 2)),
        ],
        compiler_params=pltpu.CompilerParams(
            collective_id=1, has_side_effects=True, vmem_limit_bytes=64 * 2**20
        ),
    )(tokens, masked, cotangent, live, mask_token, norm_gain, norm_shift, layer_scale, w_own, w2, table, corner, select_f, select_b)


class Share(Spread):
    def __init__(self, place, blocks, pieces, sems):
        super().__init__(place, sems)
        self.blocks, self.pieces = blocks, pieces

    def run(self, own_sem, out, out_sem):
        place, pieces = self.place, self.pieces
        at = place.at
        c, x, y, z = at["c"], at["x"], at["y"], at["z"]
        own = pltpu.make_async_copy(self.blocks.at[y], pieces.at[c, z, x, y], own_sem)
        own.start()
        for step in (1, 2, 3):
            self.send(step - 1, self.blocks.at[place.index("y", step)], pieces.at[c, z, x, y], place.go("y", step))
        own.wait()
        for step in (1, 2, 3):
            self.wait(step - 1, pieces.at[c, z, x, place.index("y", 4 - step)])
        low, high = pl.ds(0, 2), pl.ds(2, 2)
        for step in (1, 2, 3):
            self.send(2 + step, pieces.at[c, z, x, low], pieces.at[c, z, x, low], place.go("x", step))
            self.send(5 + step, pieces.at[c, z, x, high], pieces.at[c, z, x, high], place.go("z", step))
        for step in (1, 2, 3):
            self.wait(2 + step, pieces.at[c, z, place.index("x", 4 - step), low])
            self.wait(5 + step, pieces.at[c, place.index("z", 4 - step), x, high])
        row, column = pieces.at[c, z, :, low], pieces.at[c, :, x, high]
        for step in (1, 3, 2):
            self.send(8 + step, row, row, place.go("z", step))
            self.send(11 + step, column, column, place.go("x", step))
        self.send(15, row, row, place.go("c", 1))
        self.send(16, column, column, place.go("c", 1))
        for step in (1, 3, 2):
            row = pieces.at[c, place.index("z", 4 - step), :, low]
            self.wait(8 + step, row)
            self.send(16 + step, row, row, place.go("c", 1))
            column = pieces.at[c, :, place.index("x", 4 - step), high]
            self.wait(11 + step, column)
            self.send(19 + step, column, column, place.go("c", 1))
        first = pltpu.make_async_copy(pieces.at[c], out.at[c], out_sem)
        first.start()
        self.wait(15, pieces.at[1 - c, z, :, low])
        self.wait(16, pieces.at[1 - c, :, x, high])
        for step in (1, 3, 2):
            self.wait(16 + step, pieces.at[1 - c, place.index("z", 4 - step), :, low])
            self.wait(19 + step, pieces.at[1 - c, :, place.index("x", 4 - step), high])
        first.wait()
        rest = pltpu.make_async_copy(pieces.at[1 - c], out.at[1 - c], out_sem)
        rest.start()
        rest.wait()
        self.drain()


def share_kernel(blocks, out, pieces, own_sem, out_sem, sems):
    place = Place()
    meet(place)
    Share(place, blocks, pieces, sems).run(own_sem, out, out_sem)


def assemble_kernel(first, second, third, out):
    for route, ref in enumerate((first, second, third)):
        for c in range(2):
            for a3 in range(4):
                if route == 0:
                    piece = ref[c, a3, 0, 0, 0]
                elif route == 1:
                    piece = ref[c, 0, a3, 0, 0]
                else:
                    piece = ref[c, 0, 0, a3, 0]
                left = (c * 4 + a3) * 384
                out[16 * route : 16 * route + 16, left : left + 384] = piece.astype(F32)


def share_all(blocks):
    hbm = pl.BlockSpec(memory_space=pl.ANY)
    vm = pl.BlockSpec(memory_space=pltpu.VMEM)
    pieces = pl.pallas_call(
        share_kernel,
        out_shape=jax.ShapeDtypeStruct((2, 4, 4, 4, 3, 16, 384), BF16),
        in_specs=[vm],
        out_specs=hbm,
        scratch_shapes=[
            pltpu.VMEM((2, 4, 4, 4, 3, 16, 384), BF16), pltpu.SemaphoreType.DMA, pltpu.SemaphoreType.DMA,
            pltpu.SemaphoreType.DMA((2, 23)),
        ],
        compiler_params=pltpu.CompilerParams(collective_id=3, has_side_effects=True),
    )(blocks)
    return pl.pallas_call(
        assemble_kernel,
        grid=(16,),
        out_shape=jax.ShapeDtypeStruct((D, FF), F32),
        in_specs=[
            pl.BlockSpec((2, 4, 1, 1, 1, 16, 384), lambda b: (0, 0, b // 4, b % 4, 0, 0, 0)),
            pl.BlockSpec((2, 1, 4, 1, 1, 16, 384), lambda b: (0, b % 4, 0, b // 4, 1, 0, 0)),
            pl.BlockSpec((2, 1, 1, 4, 1, 16, 384), lambda b: (0, b // 4, b % 4, 0, 2, 0, 0)),
        ],
        out_specs=pl.BlockSpec((48, FF), lambda b: (b, 0)),
    )(pieces, pieces, pieces)


def on_device(
    tokens, masked, live_images, mask_token, norm_gain, norm_shift, w_first, w_second, layer_scale, rel_table, cotangent
):
    table = jnp.transpose(rel_table, (0, 2, 1)).reshape(2 * HEADS, -1)
    turned = jnp.pad(table[:, : SPAN * SPAN][:, ::-1], ((0, 0), (0, 768 - SPAN * SPAN)))
    corner = jnp.pad(table[:, SPAN * SPAN :], ((0, 0), (0, 125)))
    block_out, tokens_grad, first, second, totals = layers(
        tokens, masked, cotangent, live_images, mask_token.reshape(1, D), norm_gain, norm_shift, layer_scale,
        w_first, w_second, turned, corner,
    )
    first_grad = share_all(first)
    count = jnp.sum(live_images).astype(F32) * (SEQ * D)
    rms = jnp.sqrt(jnp.sum(totals[:8], axis=1) / count).reshape(4, 2)
    own = lax.dynamic_slice(totals, (8 + 3 * lax.axis_index("section"), 0), (3, D))
    table_grad = jnp.transpose(totals[24:].reshape(2, HEADS, D)[:, :, :732], (0, 2, 1))
    return (
        block_out, tokens_grad, first_grad[None], second,
        own[1:2], own[2:3], own[0:1], table_grad, totals[20], rms,
    )


def solution(mesh):
    both = P(("dp", "section"), None, None)
    part = P("section", None)
    return jax.shard_map(
        on_device,
        mesh=mesh,
        in_specs=(both, P(("dp", "section"), None), P(), P(), part, part, P("section", None, None), P(), part, P(), both),
        out_specs=(
            both, both, P("section", None, None), P(None, ("dp", "section"), None), part, part, part, P(), P(), P(),
        ),
        check_vma=False,
    )
```

time: 402 us -> 243 us (0.60)
  Pallas kernels: 378 us -> 228 us
  local copies, waits for them, and re-layouts: 15.4 us -> 10.5 us
    pallas_call x3 -> x1, Pallas kernels: 336 us -> 188 us  [layers(): pl.pallas_call(layers_kernel, out_shape=(jax.ShapeDtypeStruct((1, SEQ, D)...]
where the time goes in v2:
time: 243 us; the launch traced here: 242 us
  Pallas kernels  228 us (94%)
  local copies, waits for them, and re-layouts  10.5 us (4%)
    pallas_call x1, Pallas kernels, layers(): pl.pallas_call(layers_kernel, out_shape=(jax.ShapeDtypeStruct((1, SEQ, D)...  188 us
    pallas_call x1, Pallas kernels, share_all(): pl.pallas_call(share_kernel, out_shape=jax.ShapeDtypeStruct((2, 4, 4, 4,...  28.8 us
    pallas_call x1, Pallas kernels, share_all(): pl.pallas_call(assemble_kernel, grid=(16,), out_shape=jax.ShapeDtypeStruc...  11.7 us

profile of v2, /device:TPU:1, one launch (start us, length us, event | category | flops | bytes accessed | tf_op | source)
XLA Modules:
  0.0 242.3 jit_solution(3987601673606397104)
XLA Ops:
  0.6 1.3 reduce_sum.19
  2.6 1.3 reshape.34.mask_token
  3.9 0.9 copy.26
  4.8 0.1 slice.37
  4.8 0.6 pad.9.corner
  5.5 0.4 reverse
  5.9 0.1 slice.42
  6.0 0.7 pad.8.table
  6.6 187.7 %shard_map.204 = (bf16[1,197,768]{2,1,0:T(8,128)(2,1)}, bf16[1,197,768]{2,1,0:T(8,128)(2,1)}, bf16[4,3,16,384]{3,2,1,0:T(8,128)(2,1)}, f32[2,24,768]{2,1,0:T(8,128)}, f32[48,768]{1,0:T(8,128)}) custom-call(bf16[1,197,768]{2,1,0:T(8,128)(2,1)} %tokens.1, s32[1,197]{1,0:T(1,128)} %masked.1, bf16[1,197,768]{2,1,0:T(8,128)(2,1)} %cotangent.1, s32[32]{0:T(128)} %live.1, ...), custom_call_target="tpu_custom_call" | custom-call | tf_op jit(solution)/shard_map/pallas_call | solution.py:819
  194.4 0.9 slice_reduce_fusion
  195.2 0.1 sqrt.8
  195.3 0.7 copy.28
  196.0 2.0 slice_reduce_fusion.1
  198.0 0.9 slice.32
  198.9 0.7 copy.27
  199.6 28.8 %shard_map.205.first.second.third = bf16[2,4,4,4,3,16,384]{6,5,4,3,2,1,0:T(8,128)(2,1)} custom-call(bf16[4,3,16,384]{3,2,1,0:T(8,128)(2,1)} %get-tuple-element.17.blocks), custom_call_target="tpu_custom_call" | custom-call | tf_op jit(solution)/shard_map/pallas_call | solution.py:921
  228.5 0.0 copy-start.1
  228.5 0.0 copy-start
  228.5 0.0 copy-start.2
  228.5 11.7 %shard_map.206 = f32[768,3072]{1,0:T(8,128)} custom-call(bf16[2,4,4,4,3,16,384]{6,5,4,3,2,1,0:T(8,128)(2,1)} %shard_map.205.first.second.third, bf16[2,4,4,4,3,16,384]{6,5,4,3,2,1,0:T(8,128)(2,1)} %shard_map.205.first.second.third, bf16[2,4,4,4,3,16,384]{6,5,4,3,2,1,0:T(8,128)(2,1)} %shard_map.205.first.second.third), custom_call_target="tpu_custom_call" | custom-call | tf_op jit(solution)/shard_map/pallas_call | solution.py:932
  240.2 0.0 copy-done.1
  240.2 0.7 copy.32
  240.9 0.0 copy-done
  240.9 0.7 copy.33
  241.6 0.0 copy-done.2
  241.6 0.7 copy.34
  (4 shorter events, 0.0 us)
Async XLA Ops:
  228.5 11.7 %copy-start.1 = (bf16[1,197,768]{2,1,0:T(8,128)(2,1)S(1)}, bf16[1,197,768]{2,1,0:T(8,128)(2,1)}, u32[]{:S(2)}) copy-start(bf16[1,197,768]{2,1,0:T(8,128)(2,1)} %get-tuple-element.54) | copy-start | bytes 907780
  228.5 12.4 %copy-start = (bf16[1,197,768]{2,1,0:T(8,128)(2,1)S(1)}, bf16[1,197,768]{2,1,0:T(8,128)(2,1)}, u32[]{:S(2)}) copy-start(bf16[1,197,768]{2,1,0:T(8,128)(2,1)} %get-tuple-element.55) | copy-start | bytes 907780
  228.5 13.1 %copy-start.2 = (f32[2,24,768]{2,1,0:T(8,128)S(1)}, f32[2,24,768]{2,1,0:T(8,128)}, u32[]{:S(2)}) copy-start(f32[2,24,768]{2,1,0:T(8,128)} %get-tuple-element.57) | copy-start | bytes 442372
